TPU v7x, 512 devices: a whole 4x8x8 slice. The times are simulated.
512 devices in a mesh: tile: 128 (over z, y, core), sub: 4 (over x).
Axes of the slice: x: 4, y: 8, z: 8, core: 2. Of those that a mesh axis runs over, the one named last changes fastest.
Arguments:
- right_side: float32 [10, 16, 512, 512], P(None, None, 'tile', 'sub'), may hold values from -24 to 24
- fine_coeffs: float32 [5, 10, 10, 512, 512], P(None, None, None, 'tile', 'sub')
- fine_inverse: float32 [10, 10, 512, 512], P(None, None, 'tile', 'sub')
- aggregate: int32 [512, 512], P('tile', 'sub'), may hold values from 0 to 63, as said below
- coarse_coeffs: float32 [5, 10, 10, 32768], P(None, None, None, 'tile')
- coarse_inverse: float32 [10, 10, 32768], P(None, None, 'tile')
- coarse_cols: int32 [5, 32768], P(None, 'tile'), may hold values from 0 to 319, as said below
- send_rows: int32 [2, 4096], P(None, 'tile'), may hold values from 0 to 207, as said below
Outputs:
- solution: float32 [10, 16, 512, 512], P(None, None, 'tile', 'sub')
Inputs may be any that keep to these rules, and one draw needn't show every extreme that they name: On each device the aggregate numbers in use are 0 to n - 1, each held by one or more cells, with n = 64 on the devices of sub index 0, 32 at index 1 and 16 at higher indices. `coarse_cols`: entry 0 of every row is the row itself within its group. Rows that no cell maps to name only themselves, and no other row names them; the other entries name such live rows of the group (below 256) or received rows (256 and above). `send_rows`: every entry is a live row of its group, as numbered within the group, a row that some cell maps to.
All inputs are finite; a program needn't handle non-finite values.
Results may differ from a plain program's by a relative error of at most 0.00007.
Values sent between devices are 32-bit elements; how exact they have to be, the bound alone decides.
No kernel may reach another device: no remote copies, remote signals or barrier semaphores. Data moves between devices by JAX's collectives and lax.ppermute only.
A program may use at most 128 MiB of HBM per device.

v0:
```python
import jax
import jax.numpy as jnp
from jax import lax
from jax.experimental import pallas as pl
from jax.experimental.pallas import tpu as pltpu
from jax.sharding import PartitionSpec as P

CSWEEP = 4
OMEGA = 0.7
THETA = 0.6
FC = 160
SLABS = 5
NIJ = 504
IJ = 104
EDGE = 176
F32 = jnp.float32
I32 = jnp.int32

VM = pl.BlockSpec(memory_space=pltpu.VMEM)
SM = pl.BlockSpec(memory_space=pltpu.SMEM)


def lanes():
    return lax.broadcasted_iota(I32, (8, 128), 1)


def roll(value, shift):
    shift = shift % 128
    return pltpu.roll(value, shift, 1) if shift else value


def pick(value, index):
    return jnp.take_along_axis(value, index, axis=1, mode="promise_in_bounds")


def row(ref, at):
    return jnp.broadcast_to(ref[pl.ds(at, 1), :], (8, 128))


def call(kernel, outs, args, scratch=(), flops=1000000):
    specs = [SM] + [VM] * (len(args) - 1)
    return pl.pallas_call(
        kernel,
        out_shape=[jax.ShapeDtypeStruct(s, F32) for s in outs],
        in_specs=specs,
        out_specs=[VM] * len(outs),
        scratch_shapes=[pltpu.VMEM(s, F32) for s in scratch],
        compiler_params=pltpu.CompilerParams(vmem_limit_bytes=24 * 1024 * 1024),
    )(*args)


def strip_groups():
    groups = []
    for start in range(0, FC, 8):
        groups.append(("r", start))
    for start in list(range(0, 96, 8)) + [92]:
        groups.append(("j", start))
    for start in list(range(0, 496, 8)) + [492]:
        groups.append(("a", start))
    groups.append(("g", 0))
    return groups


GROUPS = strip_groups()
PACKED = (len(GROUPS) + 3) // 4 * 8


def slot_columns(lane):
    slot = lane & 7
    column = jnp.where(slot <= 2, 2 - slot, jnp.where(slot >= 5, 132 - slot, jnp.where(slot == 3, 127, 0)))
    return column


def pack_kernel(meta, rhs, inverse, coeffs, aggregate, out):
    lane = lanes()
    index = slot_columns(lane)
    window = lane >> 3
    sources = {"r": rhs, "j": inverse, "a": coeffs}
    for q in range(PACKED // 8):
        packed = jnp.zeros((8, 128), F32)
        for k, (kind, start) in enumerate(GROUPS[4 * q : 4 * q + 4]):
            for x in range(4):
                if kind == "g":
                    block = jnp.broadcast_to(aggregate[pl.ds(x, 1), :].astype(F32), (8, 128))
                else:
                    block = sources[kind][pl.ds(4 * start + x, 8, stride=4), :]
                packed = jnp.where(window == 4 * k + x, pick(block, index), packed)
        out[pl.ds(8 * q, 8), :] = packed


def block_rows(coeff_row, vectors):
    out = []
    for i in range(10):
        pair = None
        for j in range(10):
            m = coeff_row(i, j)
            if pair is None:
                pair = [m * vectors[2 * j], m * vectors[2 * j + 1]]
            else:
                pair = [pair[0] + m * vectors[2 * j], pair[1] + m * vectors[2 * j + 1]]
        out += pair
    return out


def load_slab(ref, base):
    return [ref[pl.ds(base + 8 * b, 8), :] for b in range(20)]


def store_slab(ref, base, values):
    for b in range(20):
        ref[pl.ds(base + 8 * b, 8), :] = values[b]


def inverse_at(inverse, x, vectors):
    base = pl.multiple_of(x * IJ, 8)
    return block_rows(lambda i, j: row(inverse, base + (10 * i + j)), vectors)


def stencil_at(coeffs, shifted, x):
    total = None
    for n in range(5):
        vectors = load_slab(shifted, pl.multiple_of((n * SLABS + x) * FC, 8))
        base = pl.multiple_of(x * NIJ, 4) + 100 * n
        part = block_rows(lambda i, j: row(coeffs, base + (10 * i + j)), vectors)
        total = part if total is None else [a + b for a, b in zip(total, part)]
    return total


def write_edges(meta, vector, edge_a, edge_b):
    lane = lanes()
    odd = meta[0]
    for out, x in ((edge_a, 3 * (1 - odd)), (edge_b, 3 * odd)):
        base = pl.multiple_of(x * FC, 8)
        for b in range(20):
            out[pl.ds(8 * b, 8), :] = vector[pl.ds(base + 8 * b, 8), :]
        for h in range(2):
            packed = jnp.zeros((8, 128), F32)
            for f in range(10):
                strip = vector[pl.ds(4 * FC + 16 * f + 8 * h, 8), :]
                moved = pltpu.roll(strip, lax.rem(8 * f + 120 - 8 * x, 128), 1)
                packed = jnp.where((lane >> 3) == f, moved, packed)
            out[pl.ds(FC + 8 * h, 8), :] = packed


def shift_all(meta, vector, got_a, got_b, shifted):
    lane = lanes()
    odd = meta[0] == 1
    slot = lane & 7
    window = lane >> 3

    def put(n, x, b, value):
        shifted[pl.ds((n * SLABS + x) * FC + 8 * b, 8), :] = value

    strips = []
    for h in range(2):
        a, b = got_a[pl.ds(FC + 8 * h, 8), :], got_b[pl.ds(FC + 8 * h, 8), :]
        strips.append((jnp.where(odd, a, b), jnp.where(odd, b, a)))
    for b in range(20):
        f, h = b // 2, b % 2
        a_row, b_row = got_a[pl.ds(8 * b, 8), :], got_b[pl.ds(8 * b, 8), :]
        before, after = jnp.where(odd, a_row, b_row), jnp.where(odd, b_row, a_row)
        main = [vector[pl.ds(x * FC + 8 * b, 8), :] for x in range(4)]
        strip = vector[pl.ds(4 * FC + 8 * b, 8), :]
        strip = jnp.where(window == 0, roll(strips[h][0], -8 * f), strip)
        strip = jnp.where(window == 5, roll(strips[h][1], 40 - 8 * f), strip)
        for x in range(4):
            own = (window == x + 1) & ((slot == 3) | (slot == 4))
            strip = jnp.where(own, roll(main[x], 8 * (x + 1) + 4), strip)
        wall = [before] + main + [after]
        for x in range(4):
            put(0, x, b, main[x])
            put(1, x, b, wall[x])
            put(2, x, b, wall[x + 2])
            put(3, x, b, jnp.where(lane == 0, roll(strip, -(8 * (x + 1) + 5)), roll(main[x], 1)))
            put(4, x, b, jnp.where(lane == 127, roll(strip, 127 - (8 * (x + 1) + 2)), roll(main[x], -1)))
        put(0, 4, b, strip)
        put(1, 4, b, roll(strip, 8))
        put(2, 4, b, roll(strip, -8))
        put(3, 4, b, roll(strip, -1))
        put(4, 4, b, roll(strip, 1))


def first_kernel(meta, rhs, inverse, coeffs, got_1, got_2, coeffs_x, inverse_x, rhs_x, index_s, first, edge_a, edge_b):
    lane = lanes()
    slot = lane & 7
    window = lane >> 3
    odd = lax.rem(meta[1], 2) == 1
    inside = (window >= 1) & (window <= 4)
    needed = inside & ((slot == 1) | (slot == 2) | (slot == 5) | (slot == 6))
    for q in range(PACKED // 8):
        one, two = got_1[pl.ds(8 * q, 8), :], got_2[pl.ds(8 * q, 8), :]
        left, right = jnp.where(odd, one, two), jnp.where(odd, two, one)
        both = jnp.where(slot <= 2, right, jnp.where(slot >= 5, left, 0.0))
        for k, (kind, start) in enumerate(GROUPS[4 * q : 4 * q + 4]):
            placed = roll(both, 8 - 32 * k)
            if kind == "r":
                rhs_x[pl.ds(4 * FC + start, 8), :] = jnp.where(inside, placed, 0.0)
            elif kind == "j":
                inverse_x[pl.ds(4 * IJ + start, 8), :] = jnp.where(inside, placed, 0.0)
            elif kind == "a":
                coeffs_x[pl.ds(4 * NIJ + start, 8), :] = jnp.where(needed, placed, 0.0)
            else:
                index_s[...] = jnp.where(inside, placed, 0.0)
    for x in range(4):
        for kind, start in GROUPS:
            if kind == "r":
                rhs_x[pl.ds(x * FC + start, 8), :] = rhs[pl.ds(4 * start + x, 8, stride=4), :]
            elif kind == "j":
                inverse_x[pl.ds(x * IJ + start, 8), :] = inverse[pl.ds(4 * start + x, 8, stride=4), :]
            elif kind == "a":
                coeffs_x[pl.ds(x * NIJ + start, 8), :] = coeffs[pl.ds(4 * start + x, 8, stride=4), :]

    def at(x, carry):
        base = pl.multiple_of(x * FC, 8)
        values = inverse_at(inverse_x, x, load_slab(rhs_x, base))
        store_slab(first, base, [OMEGA * v for v in values])
        return carry

    lax.fori_loop(0, SLABS, at, 0)
    write_edges(meta, first, edge_a, edge_b)


def smooth_kernel(meta, coeffs_x, inverse_x, rhs_x, first, got_a, got_b, smoothed, edge_a, edge_b, shifted):
    shift_all(meta, first, got_a, got_b, shifted)

    def at(x, carry):
        base = pl.multiple_of(x * FC, 8)
        total = stencil_at(coeffs_x, shifted, x)
        left = [r - t for r, t in zip(load_slab(rhs_x, base), total)]
        step = inverse_at(inverse_x, x, left)
        store_slab(smoothed, base, [v + OMEGA * s for v, s in zip(load_slab(first, base), step)])
        return carry

    lax.fori_loop(0, SLABS, at, 0)
    write_edges(meta, smoothed, edge_a, edge_b)


def residual_kernel(meta, coeffs_x, inverse_x, rhs_x, smoothed, got_a, got_b, residual, scaled, edge_a, edge_b, shifted):
    shift_all(meta, smoothed, got_a, got_b, shifted)

    def at(x, carry):
        base = pl.multiple_of(x * FC, 8)
        total = stencil_at(coeffs_x, shifted, x)
        left = [r - t for r, t in zip(load_slab(rhs_x, base), total)]
        store_slab(residual, base, left)
        store_slab(scaled, base, inverse_at(inverse_x, x, left))
        return carry

    lax.fori_loop(0, SLABS, at, 0)
    write_edges(meta, scaled, edge_a, edge_b)


def gather_kernel(meta, coeffs_x, residual, scaled, aggregate, got_a, got_b, out, shifted, filtered):
    shift_all(meta, scaled, got_a, got_b, shifted)

    def at(x, carry):
        base = pl.multiple_of(x * FC, 8)
        total = stencil_at(coeffs_x, shifted, x)
        store_slab(filtered, base, [r - THETA * t for r, t in zip(load_slab(residual, base), total)])
        return carry

    lax.fori_loop(0, 4, at, 0)
    member = lax.broadcasted_iota(I32, (128, 128), 0) & 63
    summed = jnp.zeros((FC, 128), F32)
    for x in range(4):
        owner = jnp.broadcast_to(aggregate[pl.ds(x, 1), :], (128, 128))
        table = (owner == member).astype(jnp.float32).astype(jnp.bfloat16)
        rest = filtered[pl.ds(x * FC, FC), :]
        for _ in range(3):
            part = rest.astype(jnp.bfloat16)
            rest = rest - part.astype(F32)
            summed = summed + lax.dot_general(
                part, table, (((1,), (1,)), ((), ())), preferred_element_type=F32
            )
    low = lax.broadcasted_iota(I32, (80, 128), 1) < 64
    packed = jnp.where(low, summed[:80], summed[80:])
    for s in range(4):
        out[s] = packed


def live_lane(index):
    lane = jnp.where(index < 96, index, jnp.where(index < 192, index - 32, index - 80))
    return jnp.where(index >= 256, index - 128, lane)


def live(low, high, lane):
    return jnp.where(lane < 96, low, jnp.where(lane < 112, roll(high, 96), roll(high, 48)))


def send_coarse(meta, index, level, out_a, out_b):
    lane = lanes()
    odd = meta[0] == 1
    tables = []
    for d in range(2):
        four = jnp.concatenate([index[pl.ds(d, 1), :]] * 4, axis=1)
        tables.append(jnp.broadcast_to(live_lane(four), (8, 128)))
    for out, table in (
        (out_a, jnp.where(odd, tables[0], tables[1])),
        (out_b, jnp.where(odd, tables[1], tables[0])),
    ):
        for g in range(5):
            packed = jnp.zeros((8, 128), F32)
            for k in range(4):
                value = pick(level[pl.ds(8 * (4 * g + k), 8), :], table)
                packed = jnp.where((lane >> 5) == k, value, packed)
            out[pl.ds(8 * g, 8), :] = packed


def coarse_start_kernel(meta, got, coeffs, inverse, send, rhs, level, coeffs_l, inverse_l, out_a, out_b):
    lane = lanes()
    for b in range(20):
        r = 8 * (b % 10)
        up = 64 * (b // 10)
        part = [got[s, pl.ds(r, 8), :] for s in range(4)]
        value = jnp.where(lane < 64, roll(part[0], -up), roll(part[1], 64 - up))
        value = jnp.where(lane < 96, value, jnp.where(lane < 112, roll(part[2], 96 - up), roll(part[3], 112 - up)))
        rhs[pl.ds(8 * b, 8), :] = value
    lane10 = lax.broadcasted_iota(I32, (10, 128), 1)
    for i in range(10):
        inverse_l[i] = live(inverse[i, :, 0:128], inverse[i, :, 128:256], lane10)
    for n in range(5):
        for i in range(10):
            coeffs_l[n, i] = live(coeffs[n, i, :, 0:128], coeffs[n, i, :, 128:256], lane10)
    values = block_rows(lambda i, j: jnp.broadcast_to(inverse_l[i, pl.ds(j, 1), :], (8, 128)), load_slab(rhs, 0))
    store_slab(level, 0, [OMEGA * v for v in values])
    send_coarse(meta, send, level, out_a, out_b)


def sweep(meta, coeffs_l, inverse_l, cols, rhs, level, got_a, got_b):
    lane = lanes()
    odd = meta[0] == 1
    extra = []
    for g in range(5):
        a, b = got_a[pl.ds(8 * g, 8), :], got_b[pl.ds(8 * g, 8), :]
        before, after = jnp.where(odd, a, b), jnp.where(odd, b, a)
        for k in range(4):
            extra.append(jnp.where(lane < 32, roll(before, -32 * k), roll(after, 32 - 32 * k)))
    total = block_rows(lambda i, j: jnp.broadcast_to(coeffs_l[0, i, pl.ds(j, 1), :], (8, 128)), load_slab(level, 0))
    for n in range(1, 5):
        low, high = cols[pl.ds(n, 1), 0:128], cols[pl.ds(n, 1), 128:256]
        lane1 = lax.broadcasted_iota(I32, (8, 128), 1)
        index = live(jnp.broadcast_to(low, (8, 128)), jnp.broadcast_to(high, (8, 128)), lane1)
        index = live_lane(index)
        near = index & 127
        vectors = []
        for b in range(20):
            own = pick(level[pl.ds(8 * b, 8), :], near)
            vectors.append(jnp.where(index < 128, own, pick(extra[b], near)))
        part = block_rows(lambda i, j: jnp.broadcast_to(coeffs_l[n, i, pl.ds(j, 1), :], (8, 128)), vectors)
        total = [a + b for a, b in zip(total, part)]
    left = [r - t for r, t in zip(load_slab(rhs, 0), total)]
    step = block_rows(lambda i, j: jnp.broadcast_to(inverse_l[i, pl.ds(j, 1), :], (8, 128)), left)
    return [v + OMEGA * s for v, s in zip(load_slab(level, 0), step)]


def sweep_kernel(meta, coeffs_l, inverse_l, cols, send, rhs, level, got_a, got_b, out, out_a, out_b):
    store_slab(out, 0, sweep(meta, coeffs_l, inverse_l, cols, rhs, level, got_a, got_b))
    send_coarse(meta, send, out, out_a, out_b)


def last_sweep_kernel(
    meta, coeffs_l, inverse_l, cols, rhs, level, got_a, got_b, aggregate, index_s, spread, edge_a, edge_b
):
    lane = lanes()
    slot = lane & 7
    sub = meta[1]

    def offset(s):
        return jnp.where(s <= 0, 0, jnp.where(s == 1, 64, jnp.where(s == 2, 96, 112)))

    values = sweep(meta, coeffs_l, inverse_l, cols, rhs, level, got_a, got_b)
    for x in range(4):
        index = jnp.broadcast_to(aggregate[pl.ds(x, 1), :], (8, 128)) + offset(sub)
        store_slab(spread, x * FC, [pick(v, index) for v in values])
    index = index_s[...].astype(I32) + jnp.where(slot <= 2, offset(sub + 1), offset(sub - 1))
    window = lane >> 3
    inside = (window >= 1) & (window <= 4)
    there = inside & (((slot <= 2) & (sub < meta[2] - 1)) | ((slot >= 5) & (sub > 0)))
    index = jnp.minimum(index, 127)
    store_slab(spread, 4 * FC, [jnp.where(there, pick(v, index), 0.0) for v in values])
    write_edges(meta, spread, edge_a, edge_b)


def correct_kernel(meta, coeffs_x, inverse_x, spread, got_a, got_b, applied, scaled, edge_a, edge_b, shifted):
    shift_all(meta, spread, got_a, got_b, shifted)

    def at(x, carry):
        base = pl.multiple_of(x * FC, 8)
        total = stencil_at(coeffs_x, shifted, x)
        store_slab(applied, base, total)
        store_slab(scaled, base, inverse_at(inverse_x, x, total))
        return carry

    lax.fori_loop(0, SLABS, at, 0)
    write_edges(meta, scaled, edge_a, edge_b)


def last_kernel(
    meta, coeffs_x, inverse_x, smoothed, residual, spread, applied, scaled, got_a, got_b, out, shifted
):
    shift_all(meta, scaled, got_a, got_b, shifted)

    def at(x, carry):
        base = pl.multiple_of(x * FC, 8)
        total = stencil_at(coeffs_x, shifted, x)
        left = [
            r - a + THETA * t
            for r, a, t in zip(load_slab(residual, base), load_slab(applied, base), total)
        ]
        step = inverse_at(inverse_x, x, left)
        for b in range(20):
            at_row = pl.ds(base + 8 * b, 8)
            value = smoothed[at_row, :] + spread[at_row, :] - THETA * scaled[at_row, :] + OMEGA * step[b]
            out[pl.ds(32 * b + x, 8, stride=4), :] = value
        return carry

    lax.fori_loop(0, 4, at, 0)


def body(right_side, fine_coeffs, fine_inverse, aggregate, coarse_coeffs, coarse_inverse, coarse_cols, send_rows):
    tiles, subs = lax.axis_size("tile"), lax.axis_size("sub")
    me, sub = lax.axis_index("tile"), lax.axis_index("sub")
    meta = jnp.stack([lax.rem(me, 2), sub, jnp.int32(subs), jnp.int32(0)]).astype(I32)

    def swaps(count):
        both = []
        for begin in (0, 1):
            pairs = [(i, i + 1) for i in range(begin, count - 1, 2)]
            both.append(pairs + [(b, a) for a, b in pairs])
        return both

    tile_a, tile_b = swaps(tiles)
    sub_1, sub_2 = swaps(subs)

    def trade(edge_a, edge_b):
        got_b = lax.ppermute(edge_b, "tile", tile_b)
        got_a = lax.ppermute(edge_a, "tile", tile_a)
        return got_a, got_b

    rhs = right_side.reshape(640, 128)
    inverse = fine_inverse.reshape(400, 128)
    coeffs = fine_coeffs.reshape(2000, 128)
    slab, edge, small, cvec = (SLABS * FC, 128), (EDGE, 128), (40, 128), (FC, 128)
    shifts = [(5 * SLABS * FC, 128)]

    (packed,) = call(pack_kernel, [(PACKED, 128)], [meta, rhs, inverse, coeffs, aggregate])
    got_1 = lax.ppermute(packed, "sub", sub_1)
    got_2 = lax.ppermute(packed, "sub", sub_2)
    coeffs_x, inverse_x, rhs_x, index_s, first, edge_a, edge_b = call(
        first_kernel,
        [(SLABS * NIJ, 128), (SLABS * IJ, 128), slab, (8, 128), slab, edge, edge],
        [meta, rhs, inverse, coeffs, got_1, got_2],
    )
    got = trade(edge_a, edge_b)
    smoothed, edge_a, edge_b = call(
        smooth_kernel, [slab, edge, edge], [meta, coeffs_x, inverse_x, rhs_x, first, *got], shifts
    )
    got = trade(edge_a, edge_b)
    residual, scaled, edge_a, edge_b = call(
        residual_kernel, [slab, slab, edge, edge], [meta, coeffs_x, inverse_x, rhs_x, smoothed, *got], shifts
    )
    got = trade(edge_a, edge_b)
    (summed,) = call(
        gather_kernel, [(4, 80, 128)], [meta, coeffs_x, residual, scaled, aggregate, *got], shifts + [(4 * FC, 128)]
    )
    summed = lax.all_to_all(summed, "sub", 0, 0)
    group_rhs, level, coeffs_l, inverse_l, out_a, out_b = call(
        coarse_start_kernel,
        [cvec, cvec, (5, 10, 10, 128), (10, 10, 128), small, small],
        [meta, summed, coarse_coeffs, coarse_inverse, send_rows],
    )
    for _ in range(CSWEEP - 2):
        got = trade(out_a, out_b)
        level, out_a, out_b = call(
            sweep_kernel,
            [cvec, small, small],
            [meta, coeffs_l, inverse_l, coarse_cols, send_rows, group_rhs, level, *got],
        )
    got = trade(out_a, out_b)
    spread, edge_a, edge_b = call(
        last_sweep_kernel,
        [slab, edge, edge],
        [meta, coeffs_l, inverse_l, coarse_cols, group_rhs, level, *got, aggregate, index_s],
    )
    got = trade(edge_a, edge_b)
    applied, scaled, edge_a, edge_b = call(
        correct_kernel, [slab, slab, edge, edge], [meta, coeffs_x, inverse_x, spread, *got], shifts
    )
    got = trade(edge_a, edge_b)
    (out,) = call(
        last_kernel,
        [(640, 128)],
        [meta, coeffs_x, inverse_x, smoothed, residual, spread, applied, scaled, *got],
        shifts,
    )
    return out.reshape(right_side.shape)


def solution(mesh):
    in_specs = (
        P(None, None, "tile", "sub"),
        P(None, None, None, "tile", "sub"),
        P(None, None, "tile", "sub"),
        P("tile", "sub"),
        P(None, None, None, "tile"),
        P(None, None, "tile"),
        P(None, "tile"),
        P(None, "tile"),
    )
    out_specs = P(None, None, "tile", "sub")
    return jax.shard_map(body, mesh=mesh, in_specs=in_specs, out_specs=out_specs, check_vma=False)
```

profile of v0, /device:TPU:256, one launch (start us, length us, event | category | flops | bytes accessed | tf_op | source)
XLA Modules:
  0.0 139.2 jit_solution(4398390864280373951)
XLA Ops:
  0.0 0.1 pad_add_fusion.meta
  0.1 1.2 copy-done
  1.3 1.0 copy-done.1
  2.3 0.9 copy-done.3
  3.2 0.7 copy-done.6
  3.9 1.0 shard_map.82
  4.9 0.7 collective-permute-start.1
  5.6 6.1 %collective-permute-start = (f32[200,128]{1,0:T(8,128)S(1)}, f32[200,128]{1,0:T(8,128)S(1)}, u32[]{:S(2)}, u32[]{:S(2)}) collective-permute-start(f32[200,128]{1,0:T(8,128)S(1)} %shard_map.82), channel_id=1, source_target_pairs={{0,1},{2,3},{1,0},{3,2},{4,5},{6,7},{5,4},{7,6},{8,9},{10,11},{9,8... | collective-permute-start | bytes 307208 | tf_op jit(solution)/shard_map/ppermute | solution.py:447
  11.7 0.0 collective-permute-done.1.got_2
  11.7 2.6 %collective-permute-done.got_1 = f32[200,128]{1,0:T(8,128)S(1)} collective-permute-done((f32[200,128]{1,0:T(8,128)S(1)}, f32[200,128]{1,0:T(8,128)S(1)}, u32[]{:S(2)}, u32[]{:S(2)}) %collective-permute-start) | collective-permute-done | bytes 102432 | tf_op jit(solution)/shard_map/ppermute | solution.py:447
  14.3 1.2 shard_map.83
  15.5 1.9 %collective-permute-start.2 = (f32[176,128]{1,0:T(8,128)S(1)}, f32[176,128]{1,0:T(8,128)S(1)}, u32[]{:S(2)}, u32[]{:S(2)}) collective-permute-start(f32[176,128]{1,0:T(8,128)S(1)} %get-tuple-element.42), channel_id=1, source_target_pairs={{0,4},{8,12},{16,20},{24,28},{32,36},{40,44},{48,52},{56,60},{64,6... | collective-permute-start | bytes 270344 | tf_op jit(solution)/shard_map/ppermute | solution.py:437
  17.5 4.6 %collective-permute-start.3 = (f32[176,128]{1,0:T(8,128)S(1)}, f32[176,128]{1,0:T(8,128)S(1)}, u32[]{:S(2)}, u32[]{:S(2)}) collective-permute-start(f32[176,128]{1,0:T(8,128)S(1)} %get-tuple-element.43), channel_id=1, source_target_pairs={{4,8},{12,16},{20,24},{28,32},{36,40},{44,48},{52,56},{60,64},{68,... | collective-permute-start | bytes 270344 | tf_op jit(solution)/shard_map/ppermute | solution.py:436
  22.0 0.0 collective-permute-done.2.got_a
  22.1 4.6 %collective-permute-done.3.got_b = f32[176,128]{1,0:T(8,128)S(1)} collective-permute-done((f32[176,128]{1,0:T(8,128)S(1)}, f32[176,128]{1,0:T(8,128)S(1)}, u32[]{:S(2)}, u32[]{:S(2)}) %collective-permute-start.3) | collective-permute-done | bytes 90144 | tf_op jit(solution)/shard_map/ppermute | solution.py:436
  26.6 4.1 %shard_map.84 = (f32[800,128]{1,0:T(8,128)S(1)}, f32[176,128]{1,0:T(8,128)S(1)}, f32[176,128]{1,0:T(8,128)S(1)}) custom-call(s32[4]{0:T(128)S(1)} %pad_add_fusion.meta, f32[2520,128]{1,0:T(8,128)S(1)} %get-tuple-element.38.coeffs_x, f32[520,128]{1,0:T(8,128)S(1)} %get-tuple-element.39.inverse_x, f32[800,128]{1,0:T(8,128)S(1)} %get-tuple-element.40.rhs_x, ...), custom_call_target="tpu_custom_call" | custom-call | tf_op jit(solution)/shard_map/pallas_call | solution.py:42
  30.7 1.9 %collective-permute-start.4 = (f32[176,128]{1,0:T(8,128)S(1)}, f32[176,128]{1,0:T(8,128)S(1)}, u32[]{:S(2)}, u32[]{:S(2)}) collective-permute-start(f32[176,128]{1,0:T(8,128)S(1)} %get-tuple-element.45), channel_id=1, source_target_pairs={{0,4},{8,12},{16,20},{24,28},{32,36},{40,44},{48,52},{56,60},{64,6... | collective-permute-start | bytes 270344 | tf_op jit(solution)/shard_map/ppermute | solution.py:437
  32.7 4.6 %collective-permute-start.5 = (f32[176,128]{1,0:T(8,128)S(1)}, f32[176,128]{1,0:T(8,128)S(1)}, u32[]{:S(2)}, u32[]{:S(2)}) collective-permute-start(f32[176,128]{1,0:T(8,128)S(1)} %get-tuple-element.46), channel_id=1, source_target_pairs={{4,8},{12,16},{20,24},{28,32},{36,40},{44,48},{52,56},{60,64},{68,... | collective-permute-start | bytes 270344 | tf_op jit(solution)/shard_map/ppermute | solution.py:436
  37.3 4.6 %collective-permute-done.5.got_b = f32[176,128]{1,0:T(8,128)S(1)} collective-permute-done((f32[176,128]{1,0:T(8,128)S(1)}, f32[176,128]{1,0:T(8,128)S(1)}, u32[]{:S(2)}, u32[]{:S(2)}) %collective-permute-start.5) | collective-permute-done | bytes 90144 | tf_op jit(solution)/shard_map/ppermute | solution.py:436
  41.8 4.6 %shard_map.85 = (f32[800,128]{1,0:T(8,128)S(1)}, f32[800,128]{1,0:T(8,128)S(1)}, f32[176,128]{1,0:T(8,128)S(1)}, f32[176,128]{1,0:T(8,128)S(1)}) custom-call(s32[4]{0:T(128)S(1)} %pad_add_fusion.meta, f32[2520,128]{1,0:T(8,128)S(1)} %get-tuple-element.38.coeffs_x, f32[520,128]{1,0:T(8,128)S(1)} %get-tuple-element.39.inverse_x, ...), custom_call_target="tpu_custom_call" | custom-call | tf_op jit(solution)/shard_map/pallas_call | solution.py:42
  46.4 1.9 %collective-permute-start.6 = (f32[176,128]{1,0:T(8,128)S(1)}, f32[176,128]{1,0:T(8,128)S(1)}, u32[]{:S(2)}, u32[]{:S(2)}) collective-permute-start(f32[176,128]{1,0:T(8,128)S(1)} %get-tuple-element.49), channel_id=1, source_target_pairs={{0,4},{8,12},{16,20},{24,28},{32,36},{40,44},{48,52},{56,60},{64,6... | collective-permute-start | bytes 270344 | tf_op jit(solution)/shard_map/ppermute | solution.py:437
  48.4 4.6 %collective-permute-start.7 = (f32[176,128]{1,0:T(8,128)S(1)}, f32[176,128]{1,0:T(8,128)S(1)}, u32[]{:S(2)}, u32[]{:S(2)}) collective-permute-start(f32[176,128]{1,0:T(8,128)S(1)} %get-tuple-element.50), channel_id=1, source_target_pairs={{4,8},{12,16},{20,24},{28,32},{36,40},{44,48},{52,56},{60,64},{68,... | collective-permute-start | bytes 270344 | tf_op jit(solution)/shard_map/ppermute | solution.py:436
  53.0 0.0 collective-permute-done.6.got_a
  53.0 4.6 %collective-permute-done.7.got_b = f32[176,128]{1,0:T(8,128)S(1)} collective-permute-done((f32[176,128]{1,0:T(8,128)S(1)}, f32[176,128]{1,0:T(8,128)S(1)}, u32[]{:S(2)}, u32[]{:S(2)}) %collective-permute-start.7) | collective-permute-done | bytes 90144 | tf_op jit(solution)/shard_map/ppermute | solution.py:436
  57.6 4.2 %shard_map.86 = f32[4,80,128]{2,1,0:T(8,128)S(1)} custom-call(s32[4]{0:T(128)S(1)} %pad_add_fusion.meta, f32[2520,128]{1,0:T(8,128)S(1)} %get-tuple-element.38.coeffs_x, f32[800,128]{1,0:T(8,128)S(1)} %get-tuple-element.47.residual, f32[800,128]{1,0:T(8,128)S(1)} %get-tuple-element.48.scaled, s32[4,128]{1,0:T(4,128)S(1)} %copy-done.6, ...), custom_call_target="tpu_custom_call" | custom-call | tf_op jit(solution)/shard_map/pallas_call | solution.py:42
  61.7 0.0 copy-start.5
  61.8 9.8 %all_to_all.5.got = f32[4,80,128]{2,1,0:T(8,128)S(1)} all-to-all(f32[4,80,128]{2,1,0:T(8,128)S(1)} %shard_map.86), channel_id=1, replica_groups=mesh['tile'=128,'sub'=4] {'sub'}, dimensions={0} | all-to-all | bytes 327680 | tf_op jit(solution)/shard_map/all_to_all | solution.py:466
  71.6 1.1 shard_map.87
  72.7 1.9 %collective-permute-start.8 = (f32[40,128]{1,0:T(8,128)S(1)}, f32[40,128]{1,0:T(8,128)S(1)}, u32[]{:S(2)}, u32[]{:S(2)}) collective-permute-start(f32[40,128]{1,0:T(8,128)S(1)} %get-tuple-element.55), channel_id=1, source_target_pairs={{0,4},{8,12},{16,20},{24,28},{32,36},{40,44},{48,52},{56,60},{64,6... | collective-permute-start | bytes 61448 | tf_op jit(solution)/shard_map/ppermute | solution.py:437
  74.6 3.1 %collective-permute-start.9 = (f32[40,128]{1,0:T(8,128)S(1)}, f32[40,128]{1,0:T(8,128)S(1)}, u32[]{:S(2)}, u32[]{:S(2)}) collective-permute-start(f32[40,128]{1,0:T(8,128)S(1)} %get-tuple-element.56), channel_id=1, source_target_pairs={{4,8},{12,16},{20,24},{28,32},{36,40},{44,48},{52,56},{60,64},{68,... | collective-permute-start | bytes 61448 | tf_op jit(solution)/shard_map/ppermute | solution.py:436
  77.7 5.3 %collective-permute-done.9.got_b = f32[40,128]{1,0:T(8,128)S(1)} collective-permute-done((f32[40,128]{1,0:T(8,128)S(1)}, f32[40,128]{1,0:T(8,128)S(1)}, u32[]{:S(2)}, u32[]{:S(2)}) %collective-permute-start.9) | collective-permute-done | bytes 20512 | tf_op jit(solution)/shard_map/ppermute | solution.py:436
  83.0 1.4 shard_map.88
  84.4 1.9 %collective-permute-start.10 = (f32[40,128]{1,0:T(8,128)S(1)}, f32[40,128]{1,0:T(8,128)S(1)}, u32[]{:S(2)}, u32[]{:S(2)}) collective-permute-start(f32[40,128]{1,0:T(8,128)S(1)} %get-tuple-element.58), channel_id=1, source_target_pairs={{0,4},{8,12},{16,20},{24,28},{32,36},{40,44},{48,52},{56,60},{64,6... | collective-permute-start | bytes 61448 | tf_op jit(solution)/shard_map/ppermute | solution.py:437
  86.3 3.1 %collective-permute-start.11 = (f32[40,128]{1,0:T(8,128)S(1)}, f32[40,128]{1,0:T(8,128)S(1)}, u32[]{:S(2)}, u32[]{:S(2)}) collective-permute-start(f32[40,128]{1,0:T(8,128)S(1)} %get-tuple-element.59), channel_id=1, source_target_pairs={{4,8},{12,16},{20,24},{28,32},{36,40},{44,48},{52,56},{60,64},{68,... | collective-permute-start | bytes 61448 | tf_op jit(solution)/shard_map/ppermute | solution.py:436
  89.5 5.3 %collective-permute-done.11.got_b = f32[40,128]{1,0:T(8,128)S(1)} collective-permute-done((f32[40,128]{1,0:T(8,128)S(1)}, f32[40,128]{1,0:T(8,128)S(1)}, u32[]{:S(2)}, u32[]{:S(2)}) %collective-permute-start.11) | collective-permute-done | bytes 20512 | tf_op jit(solution)/shard_map/ppermute | solution.py:436
  94.7 1.4 shard_map.89
  96.1 1.9 %collective-permute-start.12 = (f32[40,128]{1,0:T(8,128)S(1)}, f32[40,128]{1,0:T(8,128)S(1)}, u32[]{:S(2)}, u32[]{:S(2)}) collective-permute-start(f32[40,128]{1,0:T(8,128)S(1)} %get-tuple-element.61), channel_id=1, source_target_pairs={{0,4},{8,12},{16,20},{24,28},{32,36},{40,44},{48,52},{56,60},{64,6... | collective-permute-start | bytes 61448 | tf_op jit(solution)/shard_map/ppermute | solution.py:437
  98.0 3.1 %collective-permute-start.13 = (f32[40,128]{1,0:T(8,128)S(1)}, f32[40,128]{1,0:T(8,128)S(1)}, u32[]{:S(2)}, u32[]{:S(2)}) collective-permute-start(f32[40,128]{1,0:T(8,128)S(1)} %get-tuple-element.62), channel_id=1, source_target_pairs={{4,8},{12,16},{20,24},{28,32},{36,40},{44,48},{52,56},{60,64},{68,... | collective-permute-start | bytes 61448 | tf_op jit(solution)/shard_map/ppermute | solution.py:436
  101.2 5.3 %collective-permute-done.13.got_b = f32[40,128]{1,0:T(8,128)S(1)} collective-permute-done((f32[40,128]{1,0:T(8,128)S(1)}, f32[40,128]{1,0:T(8,128)S(1)}, u32[]{:S(2)}, u32[]{:S(2)}) %collective-permute-start.13) | collective-permute-done | bytes 20512 | tf_op jit(solution)/shard_map/ppermute | solution.py:436
  106.4 1.5 %shard_map.90 = (f32[800,128]{1,0:T(8,128)S(1)}, f32[176,128]{1,0:T(8,128)S(1)}, f32[176,128]{1,0:T(8,128)S(1)}) custom-call(s32[4]{0:T(128)S(1)} %pad_add_fusion.meta, f32[5,10,10,128]{3,2,1,0:T(8,128)S(1)} %get-tuple-element.51.coeffs_l, f32[10,10,128]{2,1,0:T(8,128)S(1)} %get-tuple-element.52.inverse_l, s32[5,256]{1,0:T(8,128)S(1)} %copy-done.5, ...), custom_call_target="tpu_custom_call" | custom-call | tf_op jit(solution)/shard_map/pallas_call | solution.py:42
  108.0 1.9 %collective-permute-start.14 = (f32[176,128]{1,0:T(8,128)S(1)}, f32[176,128]{1,0:T(8,128)S(1)}, u32[]{:S(2)}, u32[]{:S(2)}) collective-permute-start(f32[176,128]{1,0:T(8,128)S(1)} %get-tuple-element.65), channel_id=1, source_target_pairs={{0,4},{8,12},{16,20},{24,28},{32,36},{40,44},{48,52},{56,60},{64,6... | collective-permute-start | bytes 270344 | tf_op jit(solution)/shard_map/ppermute | solution.py:437
  109.9 3.1 %collective-permute-start.15 = (f32[176,128]{1,0:T(8,128)S(1)}, f32[176,128]{1,0:T(8,128)S(1)}, u32[]{:S(2)}, u32[]{:S(2)}) collective-permute-start(f32[176,128]{1,0:T(8,128)S(1)} %get-tuple-element.66), channel_id=1, source_target_pairs={{4,8},{12,16},{20,24},{28,32},{36,40},{44,48},{52,56},{60,64},{68,... | collective-permute-start | bytes 270344 | tf_op jit(solution)/shard_map/ppermute | solution.py:436
  113.1 6.0 %collective-permute-done.15.got_b = f32[176,128]{1,0:T(8,128)S(1)} collective-permute-done((f32[176,128]{1,0:T(8,128)S(1)}, f32[176,128]{1,0:T(8,128)S(1)}, u32[]{:S(2)}, u32[]{:S(2)}) %collective-permute-start.15) | collective-permute-done | bytes 90144 | tf_op jit(solution)/shard_map/ppermute | solution.py:436
  119.1 4.6 %shard_map.91 = (f32[800,128]{1,0:T(8,128)S(1)}, f32[800,128]{1,0:T(8,128)S(1)}, f32[176,128]{1,0:T(8,128)S(1)}, f32[176,128]{1,0:T(8,128)S(1)}) custom-call(s32[4]{0:T(128)S(1)} %pad_add_fusion.meta, f32[2520,128]{1,0:T(8,128)S(1)} %get-tuple-element.38.coeffs_x, f32[520,128]{1,0:T(8,128)S(1)} %get-tuple-element.39.inverse_x, ...), custom_call_target="tpu_custom_call" | custom-call | tf_op jit(solution)/shard_map/pallas_call | solution.py:42
  123.6 1.9 %collective-permute-start.16 = (f32[176,128]{1,0:T(8,128)S(1)}, f32[176,128]{1,0:T(8,128)S(1)}, u32[]{:S(2)}, u32[]{:S(2)}) collective-permute-start(f32[176,128]{1,0:T(8,128)S(1)} %get-tuple-element.69), channel_id=1, source_target_pairs={{0,4},{8,12},{16,20},{24,28},{32,36},{40,44},{48,52},{56,60},{64,6... | collective-permute-start | bytes 270344 | tf_op jit(solution)/shard_map/ppermute | solution.py:437
  125.6 3.1 %collective-permute-start.17 = (f32[176,128]{1,0:T(8,128)S(1)}, f32[176,128]{1,0:T(8,128)S(1)}, u32[]{:S(2)}, u32[]{:S(2)}) collective-permute-start(f32[176,128]{1,0:T(8,128)S(1)} %get-tuple-element.70), channel_id=1, source_target_pairs={{4,8},{12,16},{20,24},{28,32},{36,40},{44,48},{52,56},{60,64},{68,... | collective-permute-start | bytes 270344 | tf_op jit(solution)/shard_map/ppermute | solution.py:436
  128.7 6.0 %collective-permute-done.17.got_b = f32[176,128]{1,0:T(8,128)S(1)} collective-permute-done((f32[176,128]{1,0:T(8,128)S(1)}, f32[176,128]{1,0:T(8,128)S(1)}, u32[]{:S(2)}, u32[]{:S(2)}) %collective-permute-start.17) | collective-permute-done | bytes 90144 | tf_op jit(solution)/shard_map/ppermute | solution.py:436
  134.7 4.4 %shard_map.92 = f32[640,128]{1,0:T(8,128)} custom-call(s32[4]{0:T(128)S(1)} %pad_add_fusion.meta, f32[2520,128]{1,0:T(8,128)S(1)} %get-tuple-element.38.coeffs_x, f32[520,128]{1,0:T(8,128)S(1)} %get-tuple-element.39.inverse_x, f32[800,128]{1,0:T(8,128)S(1)} %get-tuple-element.44.smoothed, f32[800,128]{1,0:T(8,128)S(1)} %get-tuple-element.47.residual, ...), custom_call_target="tpu_custom_call" | custom-call | tf_op jit(solution)/shard_map/pallas_call | solution.py:42
  (17 shorter events, 0.0 us)
Async XLA Ops:
  0.1 1.2 copy-start
  1.3 1.0 copy-start.1
  2.3 0.9 copy-start.3
  3.2 0.7 copy-start.6
  4.9 6.8 %collective-permute-start.1 = (f32[200,128]{1,0:T(8,128)S(1)}, f32[200,128]{1,0:T(8,128)S(1)}, u32[]{:S(2)}, u32[]{:S(2)}) collective-permute-start(f32[200,128]{1,0:T(8,128)S(1)} %shard_map.82), channel_id=1, source_target_pairs={{1,2},{2,1},{5,6},{6,5},{9,10},{10,9},{13,14},{14,13},{17,18},{18,... | collective-permute-start | bytes 307208 | tf_op jit(solution)/shard_map/ppermute | solution.py:448
  5.6 8.8 %collective-permute-start = (f32[200,128]{1,0:T(8,128)S(1)}, f32[200,128]{1,0:T(8,128)S(1)}, u32[]{:S(2)}, u32[]{:S(2)}) collective-permute-start(f32[200,128]{1,0:T(8,128)S(1)} %shard_map.82), channel_id=1, source_target_pairs={{0,1},{2,3},{1,0},{3,2},{4,5},{6,7},{5,4},{7,6},{8,9},{10,11},{9,8... | collective-permute-start | bytes 307208 | tf_op jit(solution)/shard_map/ppermute | solution.py:447
  15.5 6.5 %collective-permute-start.2 = (f32[176,128]{1,0:T(8,128)S(1)}, f32[176,128]{1,0:T(8,128)S(1)}, u32[]{:S(2)}, u32[]{:S(2)}) collective-permute-start(f32[176,128]{1,0:T(8,128)S(1)} %get-tuple-element.42), channel_id=1, source_target_pairs={{0,4},{8,12},{16,20},{24,28},{32,36},{40,44},{48,52},{56,60},{64,6... | collective-permute-start | bytes 270344 | tf_op jit(solution)/shard_map/ppermute | solution.py:437
  17.5 9.2 %collective-permute-start.3 = (f32[176,128]{1,0:T(8,128)S(1)}, f32[176,128]{1,0:T(8,128)S(1)}, u32[]{:S(2)}, u32[]{:S(2)}) collective-permute-start(f32[176,128]{1,0:T(8,128)S(1)} %get-tuple-element.43), channel_id=1, source_target_pairs={{4,8},{12,16},{20,24},{28,32},{36,40},{44,48},{52,56},{60,64},{68,... | collective-permute-start | bytes 270344 | tf_op jit(solution)/shard_map/ppermute | solution.py:436
  30.7 6.5 %collective-permute-start.4 = (f32[176,128]{1,0:T(8,128)S(1)}, f32[176,128]{1,0:T(8,128)S(1)}, u32[]{:S(2)}, u32[]{:S(2)}) collective-permute-start(f32[176,128]{1,0:T(8,128)S(1)} %get-tuple-element.45), channel_id=1, source_target_pairs={{0,4},{8,12},{16,20},{24,28},{32,36},{40,44},{48,52},{56,60},{64,6... | collective-permute-start | bytes 270344 | tf_op jit(solution)/shard_map/ppermute | solution.py:437
  32.7 9.2 %collective-permute-start.5 = (f32[176,128]{1,0:T(8,128)S(1)}, f32[176,128]{1,0:T(8,128)S(1)}, u32[]{:S(2)}, u32[]{:S(2)}) collective-permute-start(f32[176,128]{1,0:T(8,128)S(1)} %get-tuple-element.46), channel_id=1, source_target_pairs={{4,8},{12,16},{20,24},{28,32},{36,40},{44,48},{52,56},{60,64},{68,... | collective-permute-start | bytes 270344 | tf_op jit(solution)/shard_map/ppermute | solution.py:436
  46.4 6.5 %collective-permute-start.6 = (f32[176,128]{1,0:T(8,128)S(1)}, f32[176,128]{1,0:T(8,128)S(1)}, u32[]{:S(2)}, u32[]{:S(2)}) collective-permute-start(f32[176,128]{1,0:T(8,128)S(1)} %get-tuple-element.49), channel_id=1, source_target_pairs={{0,4},{8,12},{16,20},{24,28},{32,36},{40,44},{48,52},{56,60},{64,6... | collective-permute-start | bytes 270344 | tf_op jit(solution)/shard_map/ppermute | solution.py:437
  48.4 9.2 %collective-permute-start.7 = (f32[176,128]{1,0:T(8,128)S(1)}, f32[176,128]{1,0:T(8,128)S(1)}, u32[]{:S(2)}, u32[]{:S(2)}) collective-permute-start(f32[176,128]{1,0:T(8,128)S(1)} %get-tuple-element.50), channel_id=1, source_target_pairs={{4,8},{12,16},{20,24},{28,32},{36,40},{44,48},{52,56},{60,64},{68,... | collective-permute-start | bytes 270344 | tf_op jit(solution)/shard_map/ppermute | solution.py:436
  57.5 14.0 %copy-start.2 = (f32[5,10,10,256]{3,2,1,0:T(8,128)S(1)}, f32[5,10,10,256]{3,2,1,0:T(8,128)}, u32[]{:S(2)}) copy-start(f32[5,10,10,256]{3,2,1,0:T(8,128)} %coeffs.1) | copy-start | bytes 1536004
  57.5 14.0 %copy-start.4 = (f32[10,10,256]{2,1,0:T(8,128)S(1)}, f32[10,10,256]{2,1,0:T(8,128)}, u32[]{:S(2)}) copy-start(f32[10,10,256]{2,1,0:T(8,128)} %inverse.1) | copy-start | bytes 307204
  57.5 14.0 %copy-start.7 = (s32[2,32]{1,0:T(2,128)S(1)}, s32[2,32]{1,0:T(2,128)}, u32[]{:S(2)}) copy-start(s32[2,32]{1,0:T(2,128)} %send.5) | copy-start | bytes 772
  61.7 21.3 %copy-start.5 = (s32[5,256]{1,0:T(8,128)S(1)}, s32[5,256]{1,0:T(8,128)}, u32[]{:S(2)}) copy-start(s32[5,256]{1,0:T(8,128)} %cols.5) | copy-start | bytes 15364
  72.7 5.1 %collective-permute-start.8 = (f32[40,128]{1,0:T(8,128)S(1)}, f32[40,128]{1,0:T(8,128)S(1)}, u32[]{:S(2)}, u32[]{:S(2)}) collective-permute-start(f32[40,128]{1,0:T(8,128)S(1)} %get-tuple-element.55), channel_id=1, source_target_pairs={{0,4},{8,12},{16,20},{24,28},{32,36},{40,44},{48,52},{56,60},{64,6... | collective-permute-start | bytes 61448 | tf_op jit(solution)/shard_map/ppermute | solution.py:437
  74.6 8.4 %collective-permute-start.9 = (f32[40,128]{1,0:T(8,128)S(1)}, f32[40,128]{1,0:T(8,128)S(1)}, u32[]{:S(2)}, u32[]{:S(2)}) collective-permute-start(f32[40,128]{1,0:T(8,128)S(1)} %get-tuple-element.56), channel_id=1, source_target_pairs={{4,8},{12,16},{20,24},{28,32},{36,40},{44,48},{52,56},{60,64},{68,... | collective-permute-start | bytes 61448 | tf_op jit(solution)/shard_map/ppermute | solution.py:436
  84.4 5.1 %collective-permute-start.10 = (f32[40,128]{1,0:T(8,128)S(1)}, f32[40,128]{1,0:T(8,128)S(1)}, u32[]{:S(2)}, u32[]{:S(2)}) collective-permute-start(f32[40,128]{1,0:T(8,128)S(1)} %get-tuple-element.58), channel_id=1, source_target_pairs={{0,4},{8,12},{16,20},{24,28},{32,36},{40,44},{48,52},{56,60},{64,6... | collective-permute-start | bytes 61448 | tf_op jit(solution)/shard_map/ppermute | solution.py:437
  86.3 8.4 %collective-permute-start.11 = (f32[40,128]{1,0:T(8,128)S(1)}, f32[40,128]{1,0:T(8,128)S(1)}, u32[]{:S(2)}, u32[]{:S(2)}) collective-permute-start(f32[40,128]{1,0:T(8,128)S(1)} %get-tuple-element.59), channel_id=1, source_target_pairs={{4,8},{12,16},{20,24},{28,32},{36,40},{44,48},{52,56},{60,64},{68,... | collective-permute-start | bytes 61448 | tf_op jit(solution)/shard_map/ppermute | solution.py:436
  96.1 5.1 %collective-permute-start.12 = (f32[40,128]{1,0:T(8,128)S(1)}, f32[40,128]{1,0:T(8,128)S(1)}, u32[]{:S(2)}, u32[]{:S(2)}) collective-permute-start(f32[40,128]{1,0:T(8,128)S(1)} %get-tuple-element.61), channel_id=1, source_target_pairs={{0,4},{8,12},{16,20},{24,28},{32,36},{40,44},{48,52},{56,60},{64,6... | collective-permute-start | bytes 61448 | tf_op jit(solution)/shard_map/ppermute | solution.py:437
  98.0 8.4 %collective-permute-start.13 = (f32[40,128]{1,0:T(8,128)S(1)}, f32[40,128]{1,0:T(8,128)S(1)}, u32[]{:S(2)}, u32[]{:S(2)}) collective-permute-start(f32[40,128]{1,0:T(8,128)S(1)} %get-tuple-element.62), channel_id=1, source_target_pairs={{4,8},{12,16},{20,24},{28,32},{36,40},{44,48},{52,56},{60,64},{68,... | collective-permute-start | bytes 61448 | tf_op jit(solution)/shard_map/ppermute | solution.py:436
  108.0 5.1 %collective-permute-start.14 = (f32[176,128]{1,0:T(8,128)S(1)}, f32[176,128]{1,0:T(8,128)S(1)}, u32[]{:S(2)}, u32[]{:S(2)}) collective-permute-start(f32[176,128]{1,0:T(8,128)S(1)} %get-tuple-element.65), channel_id=1, source_target_pairs={{0,4},{8,12},{16,20},{24,28},{32,36},{40,44},{48,52},{56,60},{64,6... | collective-permute-start | bytes 270344 | tf_op jit(solution)/shard_map/ppermute | solution.py:437
  109.9 9.2 %collective-permute-start.15 = (f32[176,128]{1,0:T(8,128)S(1)}, f32[176,128]{1,0:T(8,128)S(1)}, u32[]{:S(2)}, u32[]{:S(2)}) collective-permute-start(f32[176,128]{1,0:T(8,128)S(1)} %get-tuple-element.66), channel_id=1, source_target_pairs={{4,8},{12,16},{20,24},{28,32},{36,40},{44,48},{52,56},{60,64},{68,... | collective-permute-start | bytes 270344 | tf_op jit(solution)/shard_map/ppermute | solution.py:436
  123.6 5.1 %collective-permute-start.16 = (f32[176,128]{1,0:T(8,128)S(1)}, f32[176,128]{1,0:T(8,128)S(1)}, u32[]{:S(2)}, u32[]{:S(2)}) collective-permute-start(f32[176,128]{1,0:T(8,128)S(1)} %get-tuple-element.69), channel_id=1, source_target_pairs={{0,4},{8,12},{16,20},{24,28},{32,36},{40,44},{48,52},{56,60},{64,6... | collective-permute-start | bytes 270344 | tf_op jit(solution)/shard_map/ppermute | solution.py:437
  125.6 9.2 %collective-permute-start.17 = (f32[176,128]{1,0:T(8,128)S(1)}, f32[176,128]{1,0:T(8,128)S(1)}, u32[]{:S(2)}, u32[]{:S(2)}) collective-permute-start(f32[176,128]{1,0:T(8,128)S(1)} %get-tuple-element.70), channel_id=1, source_target_pairs={{4,8},{12,16},{20,24},{28,32},{36,40},{44,48},{52,56},{60,64},{68,... | collective-permute-start | bytes 270344 | tf_op jit(solution)/shard_map/ppermute | solution.py:436
where the time goes:
time: 140 us; the launch traced here: 139 us
  starting transfers between devices  51.6 us (37%)
  waiting for transfers between devices  44.2 us (32%)
  Pallas kernels  29.4 us (21%)
  blocking collectives  9.81 us (7%)
  local copies, waits for them, and re-layouts  3.82 us (3%)
    ppermute x8, waiting for transfers between devices, trade(): got_b = lax.ppermute(edge_b, 'tile', tile_b)  41.5 us
    ppermute x8, starting transfers between devices, trade(): got_b = lax.ppermute(edge_b, 'tile', tile_b)  29.4 us
    pallas_call x11, Pallas kernels, call(): pl.pallas_call(kernel, out_shape=[jax.ShapeDtypeStruct(s, F32) for s in o...  29.4 us
    ppermute x8, starting transfers between devices, trade(): got_a = lax.ppermute(edge_a, 'tile', tile_a)  15.4 us
    all_to_all x1, blocking collectives, body(): summed = lax.all_to_all(summed, 'sub', 0, 0)  9.81 us
    ppermute x1, starting transfers between devices, body(): got_1 = lax.ppermute(packed, 'sub', sub_1)  6.13 us
    unnamed x16, local copies, waits for them, and re-layouts  3.82 us
  transfers between devices with their start and end apart: 18, of which 9 were waited for; matrix products, arithmetic and copies ran while one was open for 0% of the time, Pallas kernels for 0%

commit v1 on v0

v1 whole, which is shorter than its diff:
```python
import jax
import jax.numpy as jnp
from jax import lax
from jax.experimental import pallas as pl
from jax.experimental.pallas import tpu as pltpu
from jax.sharding import PartitionSpec as P

CSWEEP = 4
OMEGA = 0.7
THETA = 0.6
FC = 160
SLABS = 11
STRIP = 10
NIJ = 504
IJ = 104
RAW_J = 3 * FC
RAW_A = RAW_J + 3 * IJ
RAW_G = RAW_A + 2 * NIJ
RAW = RAW_G + 8
F32 = jnp.float32
I32 = jnp.int32
MIB = 1024 * 1024

VM = pl.BlockSpec(memory_space=pltpu.VMEM)
HBM = pl.BlockSpec(memory_space=pltpu.HBM)


def lanes():
    return lax.broadcasted_iota(I32, (8, 128), 1)


def roll(value, shift):
    shift = shift % 128
    return pltpu.roll(value, shift, 1) if shift else value


def pick(value, index):
    return jnp.take_along_axis(value, index, axis=1, mode="promise_in_bounds")


def row(ref, at):
    return jnp.broadcast_to(ref[pl.ds(at, 1), :], (8, 128))


def spread_row(ref, at):
    return jnp.broadcast_to(ref[pl.ds(at, 1), :], (8, 128))


def odd_tile():
    return lax.rem(lax.axis_index("tile"), 2)


def call(kernel, outs, args, scratch=(), specs=None, limit=24):
    def shape(s):
        return s if isinstance(s, jax.ShapeDtypeStruct) else jax.ShapeDtypeStruct(s, F32)

    return pl.pallas_call(
        kernel,
        out_shape=[shape(s) for s in outs],
        in_specs=specs or [VM] * len(args),
        out_specs=[VM] * len(outs),
        scratch_shapes=[pltpu.VMEM(s, F32) if isinstance(s, tuple) else s for s in scratch],
        compiler_params=pltpu.CompilerParams(vmem_limit_bytes=limit * MIB),
    )(*args)


def strip_groups():
    groups = []
    for start in range(0, FC, 8):
        groups.append(("r", start))
    for start in list(range(0, 96, 8)) + [92]:
        groups.append(("j", start))
    for start in list(range(0, 496, 8)) + [492]:
        groups.append(("a", start))
    groups.append(("g", 0))
    return groups


GROUPS = strip_groups()
PACKED = (len(GROUPS) + 3) // 4 * 8


def slot_columns(lane):
    slot = lane & 7
    column = jnp.where(slot <= 2, 2 - slot, jnp.where(slot >= 5, 132 - slot, jnp.where(slot == 3, 127, 0)))
    return column


def raw_message(out, at_row, rhs, inverse, coeffs, aggregate):
    for r in range(3):
        for start in range(0, FC, 8):
            out[pl.ds(r * FC + start, 8), :] = rhs[pl.ds(4 * start + at_row + r, 8, stride=4), :]
        for start in list(range(0, 96, 8)) + [92]:
            out[pl.ds(RAW_J + r * IJ + start, 8), :] = inverse[pl.ds(4 * start + at_row + r, 8, stride=4), :]
    for r in range(2):
        for start in list(range(0, 496, 8)) + [492]:
            out[pl.ds(RAW_A + r * NIJ + start, 8), :] = coeffs[pl.ds(4 * start + 2 * at_row + r, 8, stride=4), :]
    first = jnp.where(at_row == 0, aggregate[pl.ds(0, 1), :], aggregate[pl.ds(2, 1), :])
    second = jnp.where(at_row == 0, aggregate[pl.ds(1, 1), :], aggregate[pl.ds(3, 1), :])
    sublane = lax.broadcasted_iota(I32, (8, 128), 0)
    both = jnp.where(sublane == 0, jnp.broadcast_to(first, (8, 128)), jnp.broadcast_to(second, (8, 128)))
    out[pl.ds(RAW_G, 8), :] = both.astype(F32)


def pack_kernel(rhs_in, inverse_in, coeffs_in, aggregate_in, packed_out, rhs, inverse, coeffs, aggregate, sems):
    copies = []
    for k, (source, target) in enumerate(
        ((coeffs_in, coeffs), (rhs_in, rhs), (inverse_in, inverse), (aggregate_in, aggregate))
    ):
        copies.append(pltpu.make_async_copy(source, target, sems.at[k]))
    for copy in copies:
        copy.start()
    for copy in copies:
        copy.wait()
    lane = lanes()
    index = slot_columns(lane)
    window = lane >> 3
    sources = {"r": rhs, "j": inverse, "a": coeffs}
    for q in range(PACKED // 8):
        packed = jnp.zeros((8, 128), F32)
        for k, (kind, start) in enumerate(GROUPS[4 * q : 4 * q + 4]):
            for x in range(4):
                if kind == "g":
                    block = jnp.broadcast_to(aggregate[pl.ds(x, 1), :].astype(F32), (8, 128))
                else:
                    block = sources[kind][pl.ds(4 * start + x, 8, stride=4), :]
                packed = jnp.where(window == 4 * k + x, pick(block, index), packed)
        packed_out[pl.ds(8 * q, 8), :] = packed


def raw_kernel(packed, rhs, inverse, coeffs, aggregate, raw_b, raw_a):
    odd = odd_tile()
    raw_message(raw_b, odd, rhs, inverse, coeffs, aggregate)
    raw_message(raw_a, 1 - odd, rhs, inverse, coeffs, aggregate)


def merge_kernel(got_1, got_2, mine):
    lane = lanes()
    slot = lane & 7
    odd = lax.rem(lax.axis_index("sub"), 2) == 1
    for q in range(PACKED // 8):
        one, two = got_1[pl.ds(8 * q, 8), :], got_2[pl.ds(8 * q, 8), :]
        left, right = jnp.where(odd, one, two), jnp.where(odd, two, one)
        mine[pl.ds(8 * q, 8), :] = jnp.where(slot <= 2, right, jnp.where(slot >= 5, left, 0.0))


def block_rows(coeff_row, vectors):
    out = []
    for i in range(10):
        pair = None
        for j in range(10):
            m = coeff_row(i, j)
            if pair is None:
                pair = [m * vectors[2 * j], m * vectors[2 * j + 1]]
            else:
                pair = [pair[0] + m * vectors[2 * j], pair[1] + m * vectors[2 * j + 1]]
        out += pair
    return out


def load_slab(ref, base):
    return [ref[pl.ds(base + 8 * b, 8), :] for b in range(20)]


def store_slab(ref, base, values):
    for b in range(20):
        ref[pl.ds(base + 8 * b, 8), :] = values[b]


def at_slab(x):
    return x * FC if isinstance(x, int) else pl.multiple_of(x * FC, 8)


def inverse_at(inverse, x, vectors):
    base = x * IJ if isinstance(x, int) else pl.multiple_of(x * IJ, 8)
    return block_rows(lambda i, j: row(inverse, base + (10 * i + j)), vectors)


def neighbour(source, x, n):
    base = at_slab(x)
    if isinstance(x, int) and x == STRIP:
        shift = (0, 8, -8, -1, 1)[n]
        return [roll(v, shift) for v in load_slab(source, base)]
    if n < 3:
        return load_slab(source, base + (0, -FC, FC)[n])
    lane = lanes()
    out = []
    for b in range(20):
        value = source[pl.ds(base + 8 * b, 8), :]
        strip = source[pl.ds(STRIP * FC + 8 * b, 8), :]
        if n == 3:
            out.append(jnp.where(lane == 0, pltpu.roll(strip, 123 - 8 * x, 1), roll(value, 1)))
        else:
            out.append(jnp.where(lane == 127, pltpu.roll(strip, 125 - 8 * x, 1), roll(value, -1)))
    return out


def stencil_at(coeffs, source, x):
    total = None
    if isinstance(x, int):
        base = 8 * NIJ
    else:
        base = pl.multiple_of((x - 1) * NIJ, 8)
    for n in range(5):
        vectors = neighbour(source, x, n)
        part = block_rows(lambda i, j: row(coeffs, base + (100 * n + 10 * i + j)), vectors)
        total = part if total is None else [a + b for a, b in zip(total, part)]
    return total


def copy_columns(ref, x, values):
    lane = lanes()
    own = (lane == 8 * x + 3) | (lane == 8 * x + 4)
    for b in range(20):
        at = pl.ds(STRIP * FC + 8 * b, 8)
        ref[at, :] = jnp.where(own, pltpu.roll(values[b], 8 * x + 4, 1), ref[at, :])


def over(low, high, step):
    step(STRIP)

    def at(x, carry):
        step(x)
        return carry

    lax.fori_loop(low, high + 1, at, 0)


def down_kernel(
    rhs, inverse, coeffs, aggregate, mine, raw_b, raw_a, strip_a, strip_b,
    coeffs_x, inverse_x, smoothed, residual, index_s, index_t, out,
    rhs_x, first, scaled, filtered,
):
    lane = lanes()
    slot = lane & 7
    odd = odd_tile() == 1
    needed = (lane >= 8) & (lane < 72) & ((slot == 1) | (slot == 2) | (slot == 5) | (slot == 6))
    for q in range(PACKED // 8):
        at = pl.ds(8 * q, 8)
        a, b, own = strip_a[at, :], strip_b[at, :], mine[at, :]
        before, after = jnp.where(odd, a, b), jnp.where(odd, b, a)
        for k, (kind, start) in enumerate(GROUPS[4 * q : 4 * q + 4]):
            placed = jnp.where(
                lane < 24,
                roll(before, -32 * k - 8),
                jnp.where(lane < 56, roll(own, 24 - 32 * k), roll(after, 56 - 32 * k)),
            )
            if kind == "r":
                rhs_x[pl.ds(STRIP * FC + start, 8), :] = jnp.where(lane < 80, placed, 0.0)
            elif kind == "j":
                inverse_x[pl.ds(STRIP * IJ + start, 8), :] = jnp.where(lane < 80, placed, 0.0)
            elif kind == "a":
                coeffs_x[pl.ds(8 * NIJ + start, 8), :] = jnp.where(needed, placed, 0.0)
            else:
                index_s[...] = jnp.where(lane < 80, placed, 0.0)
    for x in range(4):
        for kind, start in GROUPS:
            at = pl.ds(4 * start + x, 8, stride=4)
            if kind == "r":
                rhs_x[pl.ds((x + 3) * FC + start, 8), :] = rhs[at, :]
            elif kind == "j":
                inverse_x[pl.ds((x + 3) * IJ + start, 8), :] = inverse[at, :]
            elif kind == "a":
                coeffs_x[pl.ds((x + 2) * NIJ + start, 8), :] = coeffs[at, :]

    def outer(at_raw, count, ref, at_before, at_after):
        for start in range(0, count, 8):
            a, b = raw_a[pl.ds(at_raw + start, 8), :], raw_b[pl.ds(at_raw + start, 8), :]
            ref[pl.ds(at_before + start, 8), :] = jnp.where(odd, a, b)
            ref[pl.ds(at_after + start, 8), :] = jnp.where(odd, b, a)

    outer(0, 3 * FC, rhs_x, 0, 7 * FC)
    outer(RAW_J, 3 * IJ, inverse_x, 0, 7 * IJ)
    outer(RAW_A, 2 * NIJ, coeffs_x, 0, 6 * NIJ)
    a, b = raw_a[pl.ds(RAW_G, 8), :], raw_b[pl.ds(RAW_G, 8), :]
    sublane = lax.broadcasted_iota(I32, (8, 128), 0)
    after = jnp.where(odd, b, a)
    index_t[...] = jnp.where(sublane < 2, jnp.where(odd, a, b), pltpu.roll(after, 2, 0))

    def start_step(x):
        values = [OMEGA * v for v in inverse_at(inverse_x, x, load_slab(rhs_x, at_slab(x)))]
        store_slab(first, at_slab(x), values)
        if not isinstance(x, int):
            copy_columns(first, x, values)

    over(0, 9, start_step)

    def smooth_step(x):
        base = at_slab(x)
        total = stencil_at(coeffs_x, first, x)
        left = [r - t for r, t in zip(load_slab(rhs_x, base), total)]
        step = inverse_at(inverse_x, x, left)
        values = [v + OMEGA * s for v, s in zip(load_slab(first, base), step)]
        store_slab(smoothed, base, values)
        if not isinstance(x, int):
            copy_columns(smoothed, x, values)

    over(1, 8, smooth_step)

    def residual_step(x):
        base = at_slab(x)
        total = stencil_at(coeffs_x, smoothed, x)
        store_slab(residual, base, [r - t for r, t in zip(load_slab(rhs_x, base), total)])
        store_slab(scaled, base, inverse_at(inverse_x, x, load_slab(residual, base)))

    over(2, 7, residual_step)

    def filter_step(x, carry):
        base = at_slab(x)
        total = stencil_at(coeffs_x, scaled, x)
        store_slab(filtered, at_slab(x - 3), [r - THETA * t for r, t in zip(load_slab(residual, base), total)])
        return carry

    lax.fori_loop(3, 7, filter_step, 0)
    member = lax.broadcasted_iota(I32, (128, 128), 0) & 63
    summed = jnp.zeros((FC, 128), F32)
    for x in range(4):
        owner = jnp.broadcast_to(aggregate[pl.ds(x, 1), :], (128, 128))
        table = (owner == member).astype(F32).astype(jnp.bfloat16)
        rest = filtered[pl.ds(x * FC, FC), :]
        for _ in range(3):
            part = rest.astype(jnp.bfloat16)
            rest = rest - part.astype(F32)
            summed = summed + lax.dot_general(
                part, table, (((1,), (1,)), ((), ())), preferred_element_type=F32
            )
    low = lax.broadcasted_iota(I32, (80, 128), 1) < 64
    packed = jnp.where(low, summed[:80], summed[80:])
    for s in range(4):
        out[s] = packed


def live_lane(index):
    lane = jnp.where(index < 96, index, jnp.where(index < 192, index - 32, index - 80))
    return jnp.where(index >= 256, index - 128, lane)


def live(low, high, lane):
    return jnp.where(lane < 96, low, jnp.where(lane < 112, roll(high, 96), roll(high, 48)))


def send_coarse(index, level, out_a, out_b):
    lane = lanes()
    odd = odd_tile() == 1
    tables = []
    for d in range(2):
        four = jnp.concatenate([index[pl.ds(d, 1), :]] * 4, axis=1)
        tables.append(jnp.broadcast_to(live_lane(four), (8, 128)))
    for out, table in (
        (out_a, jnp.where(odd, tables[0], tables[1])),
        (out_b, jnp.where(odd, tables[1], tables[0])),
    ):
        for g in range(5):
            packed = jnp.zeros((8, 128), F32)
            for k in range(4):
                value = pick(level[pl.ds(8 * (4 * g + k), 8), :], table)
                packed = jnp.where((lane >> 5) == k, value, packed)
            out[pl.ds(8 * g, 8), :] = packed


def coarse_start_kernel(got, coeffs, inverse, send, rhs, level, coeffs_l, inverse_l, out_a, out_b):
    lane = lanes()
    for b in range(20):
        r = 8 * (b % 10)
        up = 64 * (b // 10)
        part = [got[s, pl.ds(r, 8), :] for s in range(4)]
        value = jnp.where(lane < 64, roll(part[0], -up), roll(part[1], 64 - up))
        value = jnp.where(lane < 96, value, jnp.where(lane < 112, roll(part[2], 96 - up), roll(part[3], 112 - up)))
        rhs[pl.ds(8 * b, 8), :] = value
    lane10 = lax.broadcasted_iota(I32, (10, 128), 1)
    for i in range(10):
        inverse_l[i] = live(inverse[i, :, 0:128], inverse[i, :, 128:256], lane10)
    for n in range(5):
        for i in range(10):
            coeffs_l[n, i] = live(coeffs[n, i, :, 0:128], coeffs[n, i, :, 128:256], lane10)
    values = block_rows(lambda i, j: jnp.broadcast_to(inverse_l[i, pl.ds(j, 1), :], (8, 128)), load_slab(rhs, 0))
    store_slab(level, 0, [OMEGA * v for v in values])
    send_coarse(send, level, out_a, out_b)


def sweep(coeffs_l, inverse_l, cols, rhs, level, got_a, got_b):
    lane = lanes()
    odd = odd_tile() == 1
    extra = []
    for g in range(5):
        a, b = got_a[pl.ds(8 * g, 8), :], got_b[pl.ds(8 * g, 8), :]
        before, after = jnp.where(odd, a, b), jnp.where(odd, b, a)
        for k in range(4):
            extra.append(jnp.where(lane < 32, roll(before, -32 * k), roll(after, 32 - 32 * k)))
    total = block_rows(lambda i, j: jnp.broadcast_to(coeffs_l[0, i, pl.ds(j, 1), :], (8, 128)), load_slab(level, 0))
    for n in range(1, 5):
        low, high = cols[pl.ds(n, 1), 0:128], cols[pl.ds(n, 1), 128:256]
        lane1 = lax.broadcasted_iota(I32, (8, 128), 1)
        index = live(jnp.broadcast_to(low, (8, 128)), jnp.broadcast_to(high, (8, 128)), lane1)
        index = live_lane(index)
        near = index & 127
        vectors = []
        for b in range(20):
            own = pick(level[pl.ds(8 * b, 8), :], near)
            vectors.append(jnp.where(index < 128, own, pick(extra[b], near)))
        part = block_rows(lambda i, j: jnp.broadcast_to(coeffs_l[n, i, pl.ds(j, 1), :], (8, 128)), vectors)
        total = [a + b for a, b in zip(total, part)]
    left = [r - t for r, t in zip(load_slab(rhs, 0), total)]
    step = block_rows(lambda i, j: jnp.broadcast_to(inverse_l[i, pl.ds(j, 1), :], (8, 128)), left)
    return [v + OMEGA * s for v, s in zip(load_slab(level, 0), step)]


def sweep_kernel(coeffs_l, inverse_l, cols, send, rhs, level, got_b, got_a, out, out_b, out_a):
    store_slab(out, 0, sweep(coeffs_l, inverse_l, cols, rhs, level, got_a, got_b))
    send_coarse(send, out, out_a, out_b)


def last_sweep_kernel(coeffs_l, inverse_l, cols, rhs, level, got_b, got_a, out):
    store_slab(out, 0, sweep(coeffs_l, inverse_l, cols, rhs, level, got_a, got_b))


def up_kernel(
    coeffs_x, inverse_x, smoothed, residual, aggregate, index_s, index_t, level, got_a, got_b,
    out, spread, applied, scaled,
):
    lane = lanes()
    slot = lane & 7
    odd = odd_tile() == 1
    sub, subs = lax.axis_index("sub"), lax.axis_size("sub")

    def offset(s):
        return jnp.where(s <= 0, 0, jnp.where(s == 1, 64, jnp.where(s == 2, 96, 112)))

    own_at = offset(sub)
    mains = [jnp.minimum(jnp.broadcast_to(aggregate[pl.ds(x, 1), :], (8, 128)) + own_at, 127) for x in range(4)]
    outers = [jnp.minimum(spread_row(index_t, r).astype(I32) + own_at, 127) for r in range(4)]
    side = jnp.where(slot <= 2, offset(sub + 1), offset(sub - 1))
    beside = jnp.minimum(index_s[...].astype(I32) + side, 127)
    there = ((slot <= 2) & (sub < subs - 1)) | ((slot >= 5) & (sub > 0))
    for b in range(20):
        at = pl.ds(8 * b, 8)
        own, va, vb = level[at, :], got_a[at, :], got_b[at, :]
        before, after = jnp.where(odd, va, vb), jnp.where(odd, vb, va)
        strip = jnp.where(
            lane < 24, pick(before, beside), jnp.where(lane < 56, pick(own, beside), pick(after, beside))
        )
        strip = jnp.where(there & (lane < 80), strip, 0.0)
        for x in range(1, 9):
            if x < 3:
                value = pick(before, outers[x - 1])
            elif x < 7:
                value = pick(own, mains[x - 3])
            else:
                value = pick(after, outers[x - 5])
            spread[pl.ds(x * FC + 8 * b, 8), :] = value
            strip = jnp.where((lane == 8 * x + 3) | (lane == 8 * x + 4), roll(value, 8 * x + 4), strip)
        spread[pl.ds(STRIP * FC + 8 * b, 8), :] = strip

    def spread_step(x):
        base = at_slab(x)
        store_slab(applied, base, stencil_at(coeffs_x, spread, x))
        store_slab(scaled, base, inverse_at(inverse_x, x, load_slab(applied, base)))

    over(2, 7, spread_step)

    def last_step(x, carry):
        base = at_slab(x)
        total = stencil_at(coeffs_x, scaled, x)
        left = [
            r - a + THETA * t
            for r, a, t in zip(load_slab(residual, base), load_slab(applied, base), total)
        ]
        step = inverse_at(inverse_x, x, left)
        for b in range(20):
            at = pl.ds(base + 8 * b, 8)
            value = smoothed[at, :] + spread[at, :] - THETA * scaled[at, :] + OMEGA * step[b]
            out[pl.ds(32 * b + x - 3, 8, stride=4), :] = value
        return carry

    lax.fori_loop(3, 7, last_step, 0)


def body(right_side, fine_coeffs, fine_inverse, aggregate, coarse_coeffs, coarse_inverse, coarse_cols, send_rows):
    tiles, subs = lax.axis_size("tile"), lax.axis_size("sub")

    def swaps(count):
        both = []
        for begin in (0, 1):
            pairs = [(i, i + 1) for i in range(begin, count - 1, 2)]
            both.append(pairs + [(b, a) for a, b in pairs])
        return both

    tile_a, tile_b = swaps(tiles)
    sub_1, sub_2 = swaps(subs)

    def trade(to_b, to_a):
        return lax.ppermute(to_b, "tile", tile_b), lax.ppermute(to_a, "tile", tile_a)

    rhs = right_side.reshape(640, 128)
    inverse = fine_inverse.reshape(400, 128)
    coeffs = fine_coeffs.reshape(2000, 128)
    slabs, small, cvec = (SLABS * FC, 128), (40, 128), (FC, 128)
    copy = jax.ShapeDtypeStruct

    packed, rhs, inverse, coeffs, aggregate = call(
        pack_kernel,
        [(PACKED, 128), (640, 128), (400, 128), (2000, 128), copy((4, 128), I32)],
        [rhs, inverse, coeffs, aggregate],
        [pltpu.SemaphoreType.DMA((4,))],
        [HBM] * 4,
        48,
    )
    got_1 = lax.ppermute(packed, "sub", sub_1)
    got_2 = lax.ppermute(packed, "sub", sub_2)
    raw_b, raw_a = call(raw_kernel, [(RAW, 128), (RAW, 128)], [packed, rhs, inverse, coeffs, aggregate])
    raw = trade(raw_b, raw_a)
    (mine,) = call(merge_kernel, [(PACKED, 128)], [got_1, got_2])
    strips = trade(mine, mine)[::-1]
    coeffs_x, inverse_x, smoothed, residual, index_s, index_t, summed = call(
        down_kernel,
        [(9 * NIJ, 128), (SLABS * IJ, 128), slabs, slabs, (8, 128), (8, 128), (4, 80, 128)],
        [rhs, inverse, coeffs, aggregate, mine, *raw, *strips],
        [slabs, slabs, slabs, (4 * FC, 128)],
    )
    summed = lax.all_to_all(summed, "sub", 0, 0)
    group_rhs, level, coeffs_l, inverse_l, out_a, out_b = call(
        coarse_start_kernel,
        [cvec, cvec, (5, 10, 10, 128), (10, 10, 128), small, small],
        [summed, coarse_coeffs, coarse_inverse, send_rows],
    )
    for _ in range(CSWEEP - 2):
        level, out_b, out_a = call(
            sweep_kernel,
            [cvec, small, small],
            [coeffs_l, inverse_l, coarse_cols, send_rows, group_rhs, level, *trade(out_b, out_a)],
        )
    (level,) = call(
        last_sweep_kernel,
        [cvec],
        [coeffs_l, inverse_l, coarse_cols, group_rhs, level, *trade(out_b, out_a)],
    )
    (out,) = call(
        up_kernel,
        [(640, 128)],
        [coeffs_x, inverse_x, smoothed, residual, aggregate, index_s, index_t, level, *trade(level, level)[::-1]],
        [slabs, slabs, slabs],
    )
    return out.reshape(right_side.shape)


def solution(mesh):
    in_specs = (
        P(None, None, "tile", "sub"),
        P(None, None, None, "tile", "sub"),
        P(None, None, "tile", "sub"),
        P("tile", "sub"),
        P(None, None, None, "tile"),
        P(None, None, "tile"),
        P(None, "tile"),
        P(None, "tile"),
    )
    out_specs = P(None, None, "tile", "sub")
    return jax.shard_map(body, mesh=mesh, in_specs=in_specs, out_specs=out_specs, check_vma=False)
```

time: 140 us -> 96.6 us (0.69)
  waiting for transfers between devices: 44.2 us -> 19.9 us
  starting transfers between devices: 51.6 us -> 39.7 us
  Pallas kernels: 29.4 us -> 22.8 us
    ppermute x16 -> x12, waiting for transfers between devices: 41.6 us -> 16.6 us  [the longest x6 16.6 us: trade(): lax.ppermute(to_b, 'tile', tile_b)]
    ppermute x16 -> x12, starting transfers between devices: 44.8 us -> 32.9 us  [the longest x6 21.4 us: trade(): lax.ppermute(to_b, 'tile', tile_b)]
    pallas_call x11 -> x9, Pallas kernels: 29.4 us -> 22.8 us  [call(): pl.pallas_call(kernel, out_shape=[shape(s) for s in outs], in_specs=specs...]
  transfers between devices with their start and end apart: 18 -> 14, of which waited for: 9 -> 6; matrix products, arithmetic and copies ran while one was open for 0% -> 0% of each run, Pallas kernels for 0% -> 0%
where the time goes in v1:
time: 96.6 us; the launch traced here: 95.9 us
  starting transfers between devices  39.7 us (41%)
  Pallas kernels  22.8 us (24%)
  waiting for transfers between devices  19.9 us (21%)
  blocking collectives  9.53 us (10%)
  local copies, waits for them, and re-layouts  3.82 us (4%)
    pallas_call x9, Pallas kernels, call(): pl.pallas_call(kernel, out_shape=[shape(s) for s in outs], in_specs=specs...  22.8 us
    ppermute x6, starting transfers between devices, trade(): lax.ppermute(to_b, 'tile', tile_b)  21.4 us
    ppermute x6, waiting for transfers between devices, trade(): lax.ppermute(to_b, 'tile', tile_b)  16.6 us
    ppermute x6, starting transfers between devices, trade(): lax.ppermute(to_a, 'tile', tile_a)  11.5 us
    all_to_all x1, blocking collectives, body(): summed = lax.all_to_all(summed, 'sub', 0, 0)  9.53 us
    ppermute x1, starting transfers between devices, body(): got_1 = lax.ppermute(packed, 'sub', sub_1)  6.13 us
    unnamed x16, local copies, waits for them, and re-layouts  3.82 us
    ppermute x1, waiting for transfers between devices, body(): got_1 = lax.ppermute(packed, 'sub', sub_1)  3.24 us
  transfers between devices with their start and end apart: 14, of which 6 were waited for; matrix products, arithmetic and copies ran while one was open for 0% of the time, Pallas kernels for 0%

profile of v1, /device:TPU:256, one launch (start us, length us, event | category | flops | bytes accessed | tf_op | source)
XLA Modules:
  0.0 95.9 jit_solution(49685213743937340)
XLA Ops:
  0.0 1.2 %copy-done = f32[5,10,10,4,128]{4,3,2,1,0:T(4,128)S(1)} copy-done((f32[5,10,10,4,128]{4,3,2,1,0:T(4,128)S(1)}, f32[5,10,10,4,128]{4,3,2,1,0:T(4,128)}, u32[]{:S(2)}) %copy-start) | copy-done | bytes 1024024
  1.2 1.0 %copy-done.2 = f32[10,16,4,128]{3,2,1,0:T(4,128)S(1)} copy-done((f32[10,16,4,128]{3,2,1,0:T(4,128)S(1)}, f32[10,16,4,128]{3,2,1,0:T(4,128)}, u32[]{:S(2)}) %copy-start.2) | copy-done | bytes 327704
  2.2 0.9 copy-done.3
  3.1 0.7 copy-done.7
  3.8 1.2 %shard_map.82 = (f32[200,128]{1,0:T(8,128)S(1)}, f32[640,128]{1,0:T(8,128)S(1)}, f32[400,128]{1,0:T(8,128)S(1)}, f32[2000,128]{1,0:T(8,128)S(1)}, s32[4,128]{1,0:T(4,128)S(1)}) custom-call(f32[640,128]{1,0:T(8,128)S(1)} %bitcast.5, f32[400,128]{1,0:T(8,128)S(1)} %bitcast.6, f32[2000,128]{1,0:T(8,128)S(1)} %bitcast.4, s32[4,128]{1,0:T(4,128)S(1)} %copy-done.7), custom_call_target="tpu_custom_call" | custom-call | tf_op jit(solution)/shard_map/pallas_call | solution.py:57
  5.1 0.2 shard_map.84
  5.2 0.0 copy-start.1
  5.2 0.0 copy-start.4
  5.3 0.0 copy-start.6
  5.3 4.0 %collective-permute-start.2 = (f32[1808,128]{1,0:T(8,128)S(1)}, f32[1808,128]{1,0:T(8,128)S(1)}, u32[]{:S(2)}, u32[]{:S(2)}) collective-permute-start(f32[1808,128]{1,0:T(8,128)S(1)} %get-tuple-element.36), channel_id=1, source_target_pairs={{4,8},{12,16},{20,24},{28,32},{36,40},{44,48},{52,56},{60,64},{68,... | collective-permute-start | bytes 2777096 | tf_op jit(solution)/shard_map/ppermute | solution.py:492
  9.3 1.9 %collective-permute-start.3 = (f32[1808,128]{1,0:T(8,128)S(1)}, f32[1808,128]{1,0:T(8,128)S(1)}, u32[]{:S(2)}, u32[]{:S(2)}) collective-permute-start(f32[1808,128]{1,0:T(8,128)S(1)} %get-tuple-element.37), channel_id=1, source_target_pairs={{0,4},{8,12},{16,20},{24,28},{32,36},{40,44},{48,52},{56,60},{64,6... | collective-permute-start | bytes 2777096 | tf_op jit(solution)/shard_map/ppermute | solution.py:492
  11.2 0.7 collective-permute-start.1
  11.9 6.1 %collective-permute-start = (f32[200,128]{1,0:T(8,128)S(1)}, f32[200,128]{1,0:T(8,128)S(1)}, u32[]{:S(2)}, u32[]{:S(2)}) collective-permute-start(f32[200,128]{1,0:T(8,128)S(1)} %get-tuple-element.35.packed), channel_id=1, source_target_pairs={{0,1},{2,3},{1,0},{3,2},{4,5},{6,7},{5,4},{7,6},{8,9},{10,11},{9,8... | collective-permute-start | bytes 307208 | tf_op jit(solution)/shard_map/ppermute | solution.py:508
  18.1 0.0 collective-permute-done.1.got_2
  18.1 3.2 %collective-permute-done.got_1 = f32[200,128]{1,0:T(8,128)S(1)} collective-permute-done((f32[200,128]{1,0:T(8,128)S(1)}, f32[200,128]{1,0:T(8,128)S(1)}, u32[]{:S(2)}, u32[]{:S(2)}) %collective-permute-start) | collective-permute-done | bytes 102432 | tf_op jit(solution)/shard_map/ppermute | solution.py:508
  21.3 0.0 copy-start.5
  21.3 3.6 %collective-permute-start.5 = (f32[200,128]{1,0:T(8,128)S(1)}, f32[200,128]{1,0:T(8,128)S(1)}, u32[]{:S(2)}, u32[]{:S(2)}) collective-permute-start(f32[200,128]{1,0:T(8,128)S(1)} %shard_map.83.mine), channel_id=1, source_target_pairs={{4,8},{12,16},{20,24},{28,32},{36,40},{44,48},{52,56},{60,64},{68,... | collective-permute-start | bytes 307208 | tf_op jit(solution)/shard_map/ppermute | solution.py:492
  25.0 1.9 %collective-permute-start.4 = (f32[200,128]{1,0:T(8,128)S(1)}, f32[200,128]{1,0:T(8,128)S(1)}, u32[]{:S(2)}, u32[]{:S(2)}) collective-permute-start(f32[200,128]{1,0:T(8,128)S(1)} %shard_map.83.mine), channel_id=1, source_target_pairs={{0,4},{8,12},{16,20},{24,28},{32,36},{40,44},{48,52},{56,60},{64,6... | collective-permute-start | bytes 307208 | tf_op jit(solution)/shard_map/ppermute | solution.py:492
  26.9 3.7 %collective-permute-done.5.strip_b = f32[200,128]{1,0:T(8,128)S(1)} collective-permute-done((f32[200,128]{1,0:T(8,128)S(1)}, f32[200,128]{1,0:T(8,128)S(1)}, u32[]{:S(2)}, u32[]{:S(2)}) %collective-permute-start.5) | collective-permute-done | bytes 102432 | tf_op jit(solution)/shard_map/ppermute | solution.py:492
  30.6 0.0 collective-permute-done.4.strip_a
  30.6 0.0 collective-permute-done.2.raw_b
  30.6 0.0 collective-permute-done.3.raw_a
  30.7 11.2 %shard_map.85 = (f32[4536,128]{1,0:T(8,128)S(1)}, f32[1144,128]{1,0:T(8,128)S(1)}, f32[1760,128]{1,0:T(8,128)S(1)}, f32[1760,128]{1,0:T(8,128)S(1)}, f32[8,128]{...) custom-call(f32[640,128]{1,0:T(8,128)S(1)} %get-tuple-element.31.rhs, ...), custom_call_target="tpu_custom_call" | custom-call | tf_op jit(solution)/shard_map/pallas_call | solution.py:57
  41.9 9.5 %all_to_all.5.got = f32[4,80,128]{2,1,0:T(8,128)S(1)} all-to-all(f32[4,80,128]{2,1,0:T(8,128)S(1)} %get-tuple-element.44), channel_id=1, replica_groups=mesh['tile'=128,'sub'=4] {'sub'}, dimensions={0} | all-to-all | bytes 327680 | tf_op jit(solution)/shard_map/all_to_all | solution.py:520
  51.4 0.0 copy-done.1
  51.4 0.0 copy-done.4
  51.4 0.0 copy-done.6
  51.4 0.5 shard_map.86
  51.9 3.1 %collective-permute-start.6 = (f32[40,128]{1,0:T(8,128)S(1)}, f32[40,128]{1,0:T(8,128)S(1)}, u32[]{:S(2)}, u32[]{:S(2)}) collective-permute-start(f32[40,128]{1,0:T(8,128)S(1)} %get-tuple-element.49), channel_id=1, source_target_pairs={{4,8},{12,16},{20,24},{28,32},{36,40},{44,48},{52,56},{60,64},{68,... | collective-permute-start | bytes 61448 | tf_op jit(solution)/shard_map/ppermute | solution.py:492
  55.0 1.9 %collective-permute-start.7 = (f32[40,128]{1,0:T(8,128)S(1)}, f32[40,128]{1,0:T(8,128)S(1)}, u32[]{:S(2)}, u32[]{:S(2)}) collective-permute-start(f32[40,128]{1,0:T(8,128)S(1)} %get-tuple-element.50), channel_id=1, source_target_pairs={{0,4},{8,12},{16,20},{24,28},{32,36},{40,44},{48,52},{56,60},{64,6... | collective-permute-start | bytes 61448 | tf_op jit(solution)/shard_map/ppermute | solution.py:492
  56.9 3.4 %collective-permute-done.6.got_b = f32[40,128]{1,0:T(8,128)S(1)} collective-permute-done((f32[40,128]{1,0:T(8,128)S(1)}, f32[40,128]{1,0:T(8,128)S(1)}, u32[]{:S(2)}, u32[]{:S(2)}) %collective-permute-start.6) | collective-permute-done | bytes 20512 | tf_op jit(solution)/shard_map/ppermute | solution.py:492
  60.4 0.0 collective-permute-done.7.got_a
  60.4 0.8 shard_map.87
  61.2 3.5 %collective-permute-start.8 = (f32[40,128]{1,0:T(8,128)S(1)}, f32[40,128]{1,0:T(8,128)S(1)}, u32[]{:S(2)}, u32[]{:S(2)}) collective-permute-start(f32[40,128]{1,0:T(8,128)S(1)} %get-tuple-element.52), channel_id=1, source_target_pairs={{4,8},{12,16},{20,24},{28,32},{36,40},{44,48},{52,56},{60,64},{68,... | collective-permute-start | bytes 61448 | tf_op jit(solution)/shard_map/ppermute | solution.py:492
  64.7 1.9 %collective-permute-start.9 = (f32[40,128]{1,0:T(8,128)S(1)}, f32[40,128]{1,0:T(8,128)S(1)}, u32[]{:S(2)}, u32[]{:S(2)}) collective-permute-start(f32[40,128]{1,0:T(8,128)S(1)} %get-tuple-element.53), channel_id=1, source_target_pairs={{0,4},{8,12},{16,20},{24,28},{32,36},{40,44},{48,52},{56,60},{64,6... | collective-permute-start | bytes 61448 | tf_op jit(solution)/shard_map/ppermute | solution.py:492
  66.6 2.9 %collective-permute-done.8.got_b = f32[40,128]{1,0:T(8,128)S(1)} collective-permute-done((f32[40,128]{1,0:T(8,128)S(1)}, f32[40,128]{1,0:T(8,128)S(1)}, u32[]{:S(2)}, u32[]{:S(2)}) %collective-permute-start.8) | collective-permute-done | bytes 20512 | tf_op jit(solution)/shard_map/ppermute | solution.py:492
  69.6 0.0 collective-permute-done.9.got_a
  69.6 0.8 shard_map.88
  70.4 3.5 %collective-permute-start.10 = (f32[40,128]{1,0:T(8,128)S(1)}, f32[40,128]{1,0:T(8,128)S(1)}, u32[]{:S(2)}, u32[]{:S(2)}) collective-permute-start(f32[40,128]{1,0:T(8,128)S(1)} %get-tuple-element.55), channel_id=1, source_target_pairs={{4,8},{12,16},{20,24},{28,32},{36,40},{44,48},{52,56},{60,64},{68,... | collective-permute-start | bytes 61448 | tf_op jit(solution)/shard_map/ppermute | solution.py:492
  73.9 1.9 %collective-permute-start.11 = (f32[40,128]{1,0:T(8,128)S(1)}, f32[40,128]{1,0:T(8,128)S(1)}, u32[]{:S(2)}, u32[]{:S(2)}) collective-permute-start(f32[40,128]{1,0:T(8,128)S(1)} %get-tuple-element.56), channel_id=1, source_target_pairs={{0,4},{8,12},{16,20},{24,28},{32,36},{40,44},{48,52},{56,60},{64,6... | collective-permute-start | bytes 61448 | tf_op jit(solution)/shard_map/ppermute | solution.py:492
  75.9 2.9 %collective-permute-done.10.got_b = f32[40,128]{1,0:T(8,128)S(1)} collective-permute-done((f32[40,128]{1,0:T(8,128)S(1)}, f32[40,128]{1,0:T(8,128)S(1)}, u32[]{:S(2)}, u32[]{:S(2)}) %collective-permute-start.10) | collective-permute-done | bytes 20512 | tf_op jit(solution)/shard_map/ppermute | solution.py:492
  78.8 0.0 collective-permute-done.11.got_a
  78.8 0.7 shard_map.89.level
  79.5 3.5 %collective-permute-start.13 = (f32[160,128]{1,0:T(8,128)S(1)}, f32[160,128]{1,0:T(8,128)S(1)}, u32[]{:S(2)}, u32[]{:S(2)}) collective-permute-start(f32[160,128]{1,0:T(8,128)S(1)} %shard_map.89.level), channel_id=1, source_target_pairs={{4,8},{12,16},{20,24},{28,32},{36,40},{44,48},{52,56},{60,64},{68,... | collective-permute-start | bytes 245768 | tf_op jit(solution)/shard_map/ppermute | solution.py:492
  83.0 1.9 %collective-permute-start.12 = (f32[160,128]{1,0:T(8,128)S(1)}, f32[160,128]{1,0:T(8,128)S(1)}, u32[]{:S(2)}, u32[]{:S(2)}) collective-permute-start(f32[160,128]{1,0:T(8,128)S(1)} %shard_map.89.level), channel_id=1, source_target_pairs={{0,4},{8,12},{16,20},{24,28},{32,36},{40,44},{48,52},{56,60},{64,6... | collective-permute-start | bytes 245768 | tf_op jit(solution)/shard_map/ppermute | solution.py:492
  85.0 3.6 %collective-permute-done.13.got_b = f32[160,128]{1,0:T(8,128)S(1)} collective-permute-done((f32[160,128]{1,0:T(8,128)S(1)}, f32[160,128]{1,0:T(8,128)S(1)}, u32[]{:S(2)}, u32[]{:S(2)}) %collective-permute-start.13) | collective-permute-done | bytes 81952 | tf_op jit(solution)/shard_map/ppermute | solution.py:492
  88.5 0.0 collective-permute-done.12.got_a
  88.6 7.4 %shard_map.90 = f32[640,128]{1,0:T(8,128)} custom-call(f32[4536,128]{1,0:T(8,128)S(1)} %get-tuple-element.38.coeffs_x, f32[1144,128]{1,0:T(8,128)S(1)} %get-tuple-element.39.inverse_x, f32[1760,128]{1,0:T(8,128)S(1)} %get-tuple-element.40.smoothed, f32[1760,128]{1,0:T(8,128)S(1)} %get-tuple-element.41.residual, s32[4,128]{1,0:T(4,128)S(1)} %get-tuple-element.34.aggregate, ...), custom_call_target="tpu_custom_call" | custom-call | tf_op jit(solution)/shard_map/pallas_call | solution.py:57
  (6 shorter events, 0.0 us)
Async XLA Ops:
  0.0 1.2 %copy-start = (f32[5,10,10,4,128]{4,3,2,1,0:T(4,128)S(1)}, f32[5,10,10,4,128]{4,3,2,1,0:T(4,128)}, u32[]{:S(2)}) copy-start(f32[5,10,10,4,128]{4,3,2,1,0:T(4,128)} %param.9) | copy-start | bytes 3072004
  1.2 1.0 %copy-start.2 = (f32[10,16,4,128]{3,2,1,0:T(4,128)S(1)}, f32[10,16,4,128]{3,2,1,0:T(4,128)}, u32[]{:S(2)}) copy-start(f32[10,16,4,128]{3,2,1,0:T(4,128)} %param.8) | copy-start | bytes 983044
  2.2 0.9 copy-start.3
  3.1 0.7 copy-start.7
  5.2 46.2 %copy-start.1 = (f32[5,10,10,256]{3,2,1,0:T(8,128)S(1)}, f32[5,10,10,256]{3,2,1,0:T(8,128)}, u32[]{:S(2)}) copy-start(f32[5,10,10,256]{3,2,1,0:T(8,128)} %coeffs.1) | copy-start | bytes 1536004
  5.2 46.2 %copy-start.4 = (f32[10,10,256]{2,1,0:T(8,128)S(1)}, f32[10,10,256]{2,1,0:T(8,128)}, u32[]{:S(2)}) copy-start(f32[10,10,256]{2,1,0:T(8,128)} %inverse.1) | copy-start | bytes 307204
  5.3 46.1 %copy-start.6 = (s32[2,32]{1,0:T(2,128)S(1)}, s32[2,32]{1,0:T(2,128)}, u32[]{:S(2)}) copy-start(s32[2,32]{1,0:T(2,128)} %send.5) | copy-start | bytes 772
  5.3 25.4 %collective-permute-start.2 = (f32[1808,128]{1,0:T(8,128)S(1)}, f32[1808,128]{1,0:T(8,128)S(1)}, u32[]{:S(2)}, u32[]{:S(2)}) collective-permute-start(f32[1808,128]{1,0:T(8,128)S(1)} %get-tuple-element.36), channel_id=1, source_target_pairs={{4,8},{12,16},{20,24},{28,32},{36,40},{44,48},{52,56},{60,64},{68,... | collective-permute-start | bytes 2777096 | tf_op jit(solution)/shard_map/ppermute | solution.py:492
  9.3 21.3 %collective-permute-start.3 = (f32[1808,128]{1,0:T(8,128)S(1)}, f32[1808,128]{1,0:T(8,128)S(1)}, u32[]{:S(2)}, u32[]{:S(2)}) collective-permute-start(f32[1808,128]{1,0:T(8,128)S(1)} %get-tuple-element.37), channel_id=1, source_target_pairs={{0,4},{8,12},{16,20},{24,28},{32,36},{40,44},{48,52},{56,60},{64,6... | collective-permute-start | bytes 2777096 | tf_op jit(solution)/shard_map/ppermute | solution.py:492
  11.2 6.8 %collective-permute-start.1 = (f32[200,128]{1,0:T(8,128)S(1)}, f32[200,128]{1,0:T(8,128)S(1)}, u32[]{:S(2)}, u32[]{:S(2)}) collective-permute-start(f32[200,128]{1,0:T(8,128)S(1)} %get-tuple-element.35.packed), channel_id=1, source_target_pairs={{1,2},{2,1},{5,6},{6,5},{9,10},{10,9},{13,14},{14,13},{17,18},{18,... | collective-permute-start | bytes 307208 | tf_op jit(solution)/shard_map/ppermute | solution.py:509
  11.9 9.4 %collective-permute-start = (f32[200,128]{1,0:T(8,128)S(1)}, f32[200,128]{1,0:T(8,128)S(1)}, u32[]{:S(2)}, u32[]{:S(2)}) collective-permute-start(f32[200,128]{1,0:T(8,128)S(1)} %get-tuple-element.35.packed), channel_id=1, source_target_pairs={{0,1},{2,3},{1,0},{3,2},{4,5},{6,7},{5,4},{7,6},{8,9},{10,11},{9,8... | collective-permute-start | bytes 307208 | tf_op jit(solution)/shard_map/ppermute | solution.py:508
  21.3 39.0 %copy-start.5 = (s32[5,256]{1,0:T(8,128)S(1)}, s32[5,256]{1,0:T(8,128)}, u32[]{:S(2)}) copy-start(s32[5,256]{1,0:T(8,128)} %cols.5) | copy-start | bytes 15364
  21.3 9.3 %collective-permute-start.5 = (f32[200,128]{1,0:T(8,128)S(1)}, f32[200,128]{1,0:T(8,128)S(1)}, u32[]{:S(2)}, u32[]{:S(2)}) collective-permute-start(f32[200,128]{1,0:T(8,128)S(1)} %shard_map.83.mine), channel_id=1, source_target_pairs={{4,8},{12,16},{20,24},{28,32},{36,40},{44,48},{52,56},{60,64},{68,... | collective-permute-start | bytes 307208 | tf_op jit(solution)/shard_map/ppermute | solution.py:492
  25.0 5.7 %collective-permute-start.4 = (f32[200,128]{1,0:T(8,128)S(1)}, f32[200,128]{1,0:T(8,128)S(1)}, u32[]{:S(2)}, u32[]{:S(2)}) collective-permute-start(f32[200,128]{1,0:T(8,128)S(1)} %shard_map.83.mine), channel_id=1, source_target_pairs={{0,4},{8,12},{16,20},{24,28},{32,36},{40,44},{48,52},{56,60},{64,6... | collective-permute-start | bytes 307208 | tf_op jit(solution)/shard_map/ppermute | solution.py:492
  51.9 8.4 %collective-permute-start.6 = (f32[40,128]{1,0:T(8,128)S(1)}, f32[40,128]{1,0:T(8,128)S(1)}, u32[]{:S(2)}, u32[]{:S(2)}) collective-permute-start(f32[40,128]{1,0:T(8,128)S(1)} %get-tuple-element.49), channel_id=1, source_target_pairs={{4,8},{12,16},{20,24},{28,32},{36,40},{44,48},{52,56},{60,64},{68,... | collective-permute-start | bytes 61448 | tf_op jit(solution)/shard_map/ppermute | solution.py:492
  55.0 5.4 %collective-permute-start.7 = (f32[40,128]{1,0:T(8,128)S(1)}, f32[40,128]{1,0:T(8,128)S(1)}, u32[]{:S(2)}, u32[]{:S(2)}) collective-permute-start(f32[40,128]{1,0:T(8,128)S(1)} %get-tuple-element.50), channel_id=1, source_target_pairs={{0,4},{8,12},{16,20},{24,28},{32,36},{40,44},{48,52},{56,60},{64,6... | collective-permute-start | bytes 61448 | tf_op jit(solution)/shard_map/ppermute | solution.py:492
  61.2 8.4 %collective-permute-start.8 = (f32[40,128]{1,0:T(8,128)S(1)}, f32[40,128]{1,0:T(8,128)S(1)}, u32[]{:S(2)}, u32[]{:S(2)}) collective-permute-start(f32[40,128]{1,0:T(8,128)S(1)} %get-tuple-element.52), channel_id=1, source_target_pairs={{4,8},{12,16},{20,24},{28,32},{36,40},{44,48},{52,56},{60,64},{68,... | collective-permute-start | bytes 61448 | tf_op jit(solution)/shard_map/ppermute | solution.py:492
  64.7 4.9 %collective-permute-start.9 = (f32[40,128]{1,0:T(8,128)S(1)}, f32[40,128]{1,0:T(8,128)S(1)}, u32[]{:S(2)}, u32[]{:S(2)}) collective-permute-start(f32[40,128]{1,0:T(8,128)S(1)} %get-tuple-element.53), channel_id=1, source_target_pairs={{0,4},{8,12},{16,20},{24,28},{32,36},{40,44},{48,52},{56,60},{64,6... | collective-permute-start | bytes 61448 | tf_op jit(solution)/shard_map/ppermute | solution.py:492
  70.4 8.4 %collective-permute-start.10 = (f32[40,128]{1,0:T(8,128)S(1)}, f32[40,128]{1,0:T(8,128)S(1)}, u32[]{:S(2)}, u32[]{:S(2)}) collective-permute-start(f32[40,128]{1,0:T(8,128)S(1)} %get-tuple-element.55), channel_id=1, source_target_pairs={{4,8},{12,16},{20,24},{28,32},{36,40},{44,48},{52,56},{60,64},{68,... | collective-permute-start | bytes 61448 | tf_op jit(solution)/shard_map/ppermute | solution.py:492
  73.9 4.9 %collective-permute-start.11 = (f32[40,128]{1,0:T(8,128)S(1)}, f32[40,128]{1,0:T(8,128)S(1)}, u32[]{:S(2)}, u32[]{:S(2)}) collective-permute-start(f32[40,128]{1,0:T(8,128)S(1)} %get-tuple-element.56), channel_id=1, source_target_pairs={{0,4},{8,12},{16,20},{24,28},{32,36},{40,44},{48,52},{56,60},{64,6... | collective-permute-start | bytes 61448 | tf_op jit(solution)/shard_map/ppermute | solution.py:492
  79.5 9.1 %collective-permute-start.13 = (f32[160,128]{1,0:T(8,128)S(1)}, f32[160,128]{1,0:T(8,128)S(1)}, u32[]{:S(2)}, u32[]{:S(2)}) collective-permute-start(f32[160,128]{1,0:T(8,128)S(1)} %shard_map.89.level), channel_id=1, source_target_pairs={{4,8},{12,16},{20,24},{28,32},{36,40},{44,48},{52,56},{60,64},{68,... | collective-permute-start | bytes 245768 | tf_op jit(solution)/shard_map/ppermute | solution.py:492
  83.0 5.5 %collective-permute-start.12 = (f32[160,128]{1,0:T(8,128)S(1)}, f32[160,128]{1,0:T(8,128)S(1)}, u32[]{:S(2)}, u32[]{:S(2)}) collective-permute-start(f32[160,128]{1,0:T(8,128)S(1)} %shard_map.89.level), channel_id=1, source_target_pairs={{0,4},{8,12},{16,20},{24,28},{32,36},{40,44},{48,52},{56,60},{64,6... | collective-permute-start | bytes 245768 | tf_op jit(solution)/shard_map/ppermute | solution.py:492

commit v2 on v1

--- a/solution.py
+++ b/solution.py
@@ -99,19 +99,24 @@
     second = jnp.where(at_row == 0, aggregate[pl.ds(1, 1), :], aggregate[pl.ds(3, 1), :])
     sublane = lax.broadcasted_iota(I32, (8, 128), 0)
     both = jnp.where(sublane == 0, jnp.broadcast_to(first, (8, 128)), jnp.broadcast_to(second, (8, 128)))
-    out[pl.ds(RAW_G, 8), :] = both.astype(F32)
-
-
-def pack_kernel(rhs_in, inverse_in, coeffs_in, aggregate_in, packed_out, rhs, inverse, coeffs, aggregate, sems):
-    copies = []
-    for k, (source, target) in enumerate(
-        ((coeffs_in, coeffs), (rhs_in, rhs), (inverse_in, inverse), (aggregate_in, aggregate))
-    ):
-        copies.append(pltpu.make_async_copy(source, target, sems.at[k]))
-    for copy in copies:
-        copy.start()
-    for copy in copies:
-        copy.wait()
+    out[pl.ds(RAW_G, 8), :] = both
+
+
+class Rows:
+    def __init__(self, ref, first):
+        self.ref, self.first = ref, first
+
+    def __getitem__(self, index):
+        rows, columns = index
+        return self.ref[pl.ds(rows.start + self.first, rows.size, stride=rows.stride), columns]
+
+
+def parts(whole):
+    return [Rows(whole, first) for first in (0, 640, 1040, 3040)]
+
+
+def pack_kernel(whole, packed_out):
+    rhs, inverse, coeffs, aggregate = parts(whole)
     lane = lanes()
     index = slot_columns(lane)
     window = lane >> 3
@@ -121,14 +126,15 @@
         for k, (kind, start) in enumerate(GROUPS[4 * q : 4 * q + 4]):
             for x in range(4):
                 if kind == "g":
-                    block = jnp.broadcast_to(aggregate[pl.ds(x, 1), :].astype(F32), (8, 128))
+                    block = jnp.broadcast_to(aggregate[pl.ds(x, 1), :], (8, 128))
                 else:
                     block = sources[kind][pl.ds(4 * start + x, 8, stride=4), :]
                 packed = jnp.where(window == 4 * k + x, pick(block, index), packed)
         packed_out[pl.ds(8 * q, 8), :] = packed
 
 
-def raw_kernel(packed, rhs, inverse, coeffs, aggregate, raw_b, raw_a):
+def raw_kernel(packed, whole, raw_b, raw_a):
+    rhs, inverse, coeffs, aggregate = parts(whole)
     odd = odd_tile()
     raw_message(raw_b, odd, rhs, inverse, coeffs, aggregate)
     raw_message(raw_a, 1 - odd, rhs, inverse, coeffs, aggregate)
@@ -195,14 +201,17 @@
     return out
 
 
-def stencil_at(coeffs, source, x):
+def stencil_at(coeffs, source, x, moved):
     total = None
     if isinstance(x, int):
         base = 8 * NIJ
     else:
         base = pl.multiple_of((x - 1) * NIJ, 8)
+    through = range(1, 5) if isinstance(x, int) else range(3, 5)
+    for n in through:
+        store_slab(moved, (n - 1) * FC, neighbour(source, x, n))
     for n in range(5):
-        vectors = neighbour(source, x, n)
+        vectors = load_slab(moved, (n - 1) * FC) if n in through else neighbour(source, x, n)
         part = block_rows(lambda i, j: row(coeffs, base + (100 * n + 10 * i + j)), vectors)
         total = part if total is None else [a + b for a, b in zip(total, part)]
     return total
@@ -227,12 +236,13 @@
 
 
 def down_kernel(
-    rhs, inverse, coeffs, aggregate, mine, raw_b, raw_a, strip_a, strip_b,
+    whole, mine, raw_b, raw_a, strip_a, strip_b,
     coeffs_x, inverse_x, smoothed, residual, index_s, index_t, out,
-    rhs_x, first, scaled, filtered,
+    rhs_x, first, scaled, filtered, moved,
 ):
     lane = lanes()
     slot = lane & 7
+    rhs, inverse, coeffs, aggregate = parts(whole)
     odd = odd_tile() == 1
     needed = (lane >= 8) & (lane < 72) & ((slot == 1) | (slot == 2) | (slot == 5) | (slot == 6))
     for q in range(PACKED // 8):
@@ -279,27 +289,27 @@
 
     def start_step(x):
         values = [OMEGA * v for v in inverse_at(inverse_x, x, load_slab(rhs_x, at_slab(x)))]
-        store_slab(first, at_slab(x), values)
         if not isinstance(x, int):
             copy_columns(first, x, values)
+        store_slab(first, at_slab(x), values)
 
     over(0, 9, start_step)
 
     def smooth_step(x):
         base = at_slab(x)
-        total = stencil_at(coeffs_x, first, x)
+        total = stencil_at(coeffs_x, first, x, moved)
         left = [r - t for r, t in zip(load_slab(rhs_x, base), total)]
         step = inverse_at(inverse_x, x, left)
         values = [v + OMEGA * s for v, s in zip(load_slab(first, base), step)]
-        store_slab(smoothed, base, values)
         if not isinstance(x, int):
             copy_columns(smoothed, x, values)
+        store_slab(smoothed, base, values)
 
     over(1, 8, smooth_step)
 
     def residual_step(x):
         base = at_slab(x)
-        total = stencil_at(coeffs_x, smoothed, x)
+        total = stencil_at(coeffs_x, smoothed, x, moved)
         store_slab(residual, base, [r - t for r, t in zip(load_slab(rhs_x, base), total)])
         store_slab(scaled, base, inverse_at(inverse_x, x, load_slab(residual, base)))
 
@@ -307,7 +317,7 @@
 
     def filter_step(x, carry):
         base = at_slab(x)
-        total = stencil_at(coeffs_x, scaled, x)
+        total = stencil_at(coeffs_x, scaled, x, moved)
         store_slab(filtered, at_slab(x - 3), [r - THETA * t for r, t in zip(load_slab(residual, base), total)])
         return carry
 
@@ -315,7 +325,7 @@
     member = lax.broadcasted_iota(I32, (128, 128), 0) & 63
     summed = jnp.zeros((FC, 128), F32)
     for x in range(4):
-        owner = jnp.broadcast_to(aggregate[pl.ds(x, 1), :], (128, 128))
+        owner = jnp.broadcast_to(aggregate[pl.ds(x, 1), :].astype(I32), (128, 128))
         table = (owner == member).astype(F32).astype(jnp.bfloat16)
         rest = filtered[pl.ds(x * FC, FC), :]
         for _ in range(3):
@@ -415,8 +425,8 @@
 
 
 def up_kernel(
-    coeffs_x, inverse_x, smoothed, residual, aggregate, index_s, index_t, level, got_a, got_b,
-    out, spread, applied, scaled,
+    coeffs_x, inverse_x, smoothed, residual, whole, index_s, index_t, level, got_a, got_b,
+    out, spread, applied, scaled, moved,
 ):
     lane = lanes()
     slot = lane & 7
@@ -427,7 +437,8 @@
         return jnp.where(s <= 0, 0, jnp.where(s == 1, 64, jnp.where(s == 2, 96, 112)))
 
     own_at = offset(sub)
-    mains = [jnp.minimum(jnp.broadcast_to(aggregate[pl.ds(x, 1), :], (8, 128)) + own_at, 127) for x in range(4)]
+    aggregate = parts(whole)[3]
+    mains = [jnp.minimum(row(aggregate, x).astype(I32) + own_at, 127) for x in range(4)]
     outers = [jnp.minimum(spread_row(index_t, r).astype(I32) + own_at, 127) for r in range(4)]
     side = jnp.where(slot <= 2, offset(sub + 1), offset(sub - 1))
     beside = jnp.minimum(index_s[...].astype(I32) + side, 127)
@@ -453,14 +464,14 @@
 
     def spread_step(x):
         base = at_slab(x)
-        store_slab(applied, base, stencil_at(coeffs_x, spread, x))
+        store_slab(applied, base, stencil_at(coeffs_x, spread, x, moved))
         store_slab(scaled, base, inverse_at(inverse_x, x, load_slab(applied, base)))
 
     over(2, 7, spread_step)
 
     def last_step(x, carry):
         base = at_slab(x)
-        total = stencil_at(coeffs_x, scaled, x)
+        total = stencil_at(coeffs_x, scaled, x, moved)
         left = [
             r - a + THETA * t
             for r, a, t in zip(load_slab(residual, base), load_slab(applied, base), total)
@@ -495,27 +506,20 @@
     inverse = fine_inverse.reshape(400, 128)
     coeffs = fine_coeffs.reshape(2000, 128)
     slabs, small, cvec = (SLABS * FC, 128), (40, 128), (FC, 128)
-    copy = jax.ShapeDtypeStruct
-
-    packed, rhs, inverse, coeffs, aggregate = call(
-        pack_kernel,
-        [(PACKED, 128), (640, 128), (400, 128), (2000, 128), copy((4, 128), I32)],
-        [rhs, inverse, coeffs, aggregate],
-        [pltpu.SemaphoreType.DMA((4,))],
-        [HBM] * 4,
-        48,
-    )
+
+    whole = jnp.concatenate([rhs, inverse, coeffs, aggregate.astype(F32)], axis=0)
+    (packed,) = call(pack_kernel, [(PACKED, 128)], [whole])
     got_1 = lax.ppermute(packed, "sub", sub_1)
     got_2 = lax.ppermute(packed, "sub", sub_2)
-    raw_b, raw_a = call(raw_kernel, [(RAW, 128), (RAW, 128)], [packed, rhs, inverse, coeffs, aggregate])
+    raw_b, raw_a = call(raw_kernel, [(RAW, 128), (RAW, 128)], [packed, whole])
     raw = trade(raw_b, raw_a)
     (mine,) = call(merge_kernel, [(PACKED, 128)], [got_1, got_2])
     strips = trade(mine, mine)[::-1]
     coeffs_x, inverse_x, smoothed, residual, index_s, index_t, summed = call(
         down_kernel,
         [(9 * NIJ, 128), (SLABS * IJ, 128), slabs, slabs, (8, 128), (8, 128), (4, 80, 128)],
-        [rhs, inverse, coeffs, aggregate, mine, *raw, *strips],
-        [slabs, slabs, slabs, (4 * FC, 128)],
+        [whole, mine, *raw, *strips],
+        [slabs, slabs, slabs, (4 * FC, 128), (4 * FC, 128)],
     )
     summed = lax.all_to_all(summed, "sub", 0, 0)
     group_rhs, level, coeffs_l, inverse_l, out_a, out_b = call(
@@ -537,8 +541,8 @@
     (out,) = call(
         up_kernel,
         [(640, 128)],
-        [coeffs_x, inverse_x, smoothed, residual, aggregate, index_s, index_t, level, *trade(level, level)[::-1]],
-        [slabs, slabs, slabs],
+        [coeffs_x, inverse_x, smoothed, residual, whole, index_s, index_t, level, *trade(level, level)[::-1]],
+        [slabs, slabs, slabs, (4 * FC, 128)],
     )
     return out.reshape(right_side.shape)
 

time: 96.6 us -> 93.9 us (0.972)
  local copies, waits for them, and re-layouts: 3.82 us -> 0.03 us
  other arithmetic: 0 us -> 2.13 us
    unnamed x16 -> x8, local copies, waits for them, and re-layouts: 3.82 us -> 0.03 us
    concatenate x0 -> x1, other arithmetic: none -> 1.44 us  [body(): jnp.concatenate([rhs, inverse, coeffs, aggregate.astype(F32)], axis=0)]
where the time goes in v2:
time: 93.9 us; the launch traced here: 93.4 us
  starting transfers between devices  39.7 us (42%)
  Pallas kernels  21.9 us (23%)
  waiting for transfers between devices  19.9 us (21%)
  blocking collectives  9.53 us (10%)
  other arithmetic  2.13 us (2%)
    pallas_call x9, Pallas kernels, call(): pl.pallas_call(kernel, out_shape=[shape(s) for s in outs], in_specs=specs...  21.9 us
    ppermute x6, starting transfers between devices, trade(): lax.ppermute(to_b, 'tile', tile_b)  21.4 us
    ppermute x6, waiting for transfers between devices, trade(): lax.ppermute(to_b, 'tile', tile_b)  16.6 us
    ppermute x6, starting transfers between devices, trade(): lax.ppermute(to_a, 'tile', tile_a)  11.5 us
    all_to_all x1, blocking collectives, body(): summed = lax.all_to_all(summed, 'sub', 0, 0)  9.53 us
    ppermute x1, starting transfers between devices, body(): got_1 = lax.ppermute(packed, 'sub', sub_1)  6.13 us
    ppermute x1, waiting for transfers between devices, body(): got_1 = lax.ppermute(packed, 'sub', sub_1)  3.24 us
  transfers between devices with their start and end apart: 14, of which 6 were waited for; matrix products, arithmetic and copies ran while one was open for 0% of the time, Pallas kernels for 0%

profile of v2, /device:TPU:256, one launch (start us, length us, event | category | flops | bytes accessed | tf_op | source)
XLA Modules:
  0.0 93.4 jit_solution(13408150493029648396)
XLA Ops:
  0.0 0.7 convert_element_type.3
  0.7 1.4 %pad_maximum_fusion.whole = f32[3044,128]{1,0:T(8,128)S(1)} fusion(f32[4,128]{1,0:T(4,128)S(1)} %convert_element_type.3, f32[2000,128]{1,0:T(8,128)} %bitcast.4, f32[400,128]{1,0:T(8,128)} %bitcast.6, f32[640,128]{1,0:T(8,128)} %bitcast.5), kind=kLoop, calls=%fused_computation | loop fusion | flops 1168896 | bytes 3117056 | tf_op jit(solution)/shard_map/concatenate | solution.py:510
  2.1 0.5 shard_map.82.packed
  2.6 0.2 shard_map.84
  2.8 3.9 %collective-permute-start.2 = (f32[1808,128]{1,0:T(8,128)S(1)}, f32[1808,128]{1,0:T(8,128)S(1)}, u32[]{:S(2)}, u32[]{:S(2)}) collective-permute-start(f32[1808,128]{1,0:T(8,128)S(1)} %get-tuple-element.26), channel_id=1, source_target_pairs={{4,8},{12,16},{20,24},{28,32},{36,40},{44,48},{52,56},{60,64},{68,... | collective-permute-start | bytes 2777096 | tf_op jit(solution)/shard_map/ppermute | solution.py:503
  6.7 1.9 %collective-permute-start.3 = (f32[1808,128]{1,0:T(8,128)S(1)}, f32[1808,128]{1,0:T(8,128)S(1)}, u32[]{:S(2)}, u32[]{:S(2)}) collective-permute-start(f32[1808,128]{1,0:T(8,128)S(1)} %get-tuple-element.27), channel_id=1, source_target_pairs={{0,4},{8,12},{16,20},{24,28},{32,36},{40,44},{48,52},{56,60},{64,6... | collective-permute-start | bytes 2777096 | tf_op jit(solution)/shard_map/ppermute | solution.py:503
  8.6 0.7 collective-permute-start.1
  9.3 6.1 %collective-permute-start = (f32[200,128]{1,0:T(8,128)S(1)}, f32[200,128]{1,0:T(8,128)S(1)}, u32[]{:S(2)}, u32[]{:S(2)}) collective-permute-start(f32[200,128]{1,0:T(8,128)S(1)} %shard_map.82.packed), channel_id=1, source_target_pairs={{0,1},{2,3},{1,0},{3,2},{4,5},{6,7},{5,4},{7,6},{8,9},{10,11},{9,8... | collective-permute-start | bytes 307208 | tf_op jit(solution)/shard_map/ppermute | solution.py:512
  15.4 0.0 collective-permute-done.1.got_2
  15.5 3.2 %collective-permute-done.got_1 = f32[200,128]{1,0:T(8,128)S(1)} collective-permute-done((f32[200,128]{1,0:T(8,128)S(1)}, f32[200,128]{1,0:T(8,128)S(1)}, u32[]{:S(2)}, u32[]{:S(2)}) %collective-permute-start) | collective-permute-done | bytes 102432 | tf_op jit(solution)/shard_map/ppermute | solution.py:512
  18.7 0.0 copy-start
  18.7 0.0 copy-start.1
  18.7 0.0 copy-start.3
  18.8 0.0 copy-start.2
  18.8 3.8 %collective-permute-start.5 = (f32[200,128]{1,0:T(8,128)S(1)}, f32[200,128]{1,0:T(8,128)S(1)}, u32[]{:S(2)}, u32[]{:S(2)}) collective-permute-start(f32[200,128]{1,0:T(8,128)S(1)} %shard_map.83.mine), channel_id=1, source_target_pairs={{4,8},{12,16},{20,24},{28,32},{36,40},{44,48},{52,56},{60,64},{68,... | collective-permute-start | bytes 307208 | tf_op jit(solution)/shard_map/ppermute | solution.py:503
  22.5 1.9 %collective-permute-start.4 = (f32[200,128]{1,0:T(8,128)S(1)}, f32[200,128]{1,0:T(8,128)S(1)}, u32[]{:S(2)}, u32[]{:S(2)}) collective-permute-start(f32[200,128]{1,0:T(8,128)S(1)} %shard_map.83.mine), channel_id=1, source_target_pairs={{0,4},{8,12},{16,20},{24,28},{32,36},{40,44},{48,52},{56,60},{64,6... | collective-permute-start | bytes 307208 | tf_op jit(solution)/shard_map/ppermute | solution.py:503
  24.5 3.7 %collective-permute-done.5.strip_b = f32[200,128]{1,0:T(8,128)S(1)} collective-permute-done((f32[200,128]{1,0:T(8,128)S(1)}, f32[200,128]{1,0:T(8,128)S(1)}, u32[]{:S(2)}, u32[]{:S(2)}) %collective-permute-start.5) | collective-permute-done | bytes 102432 | tf_op jit(solution)/shard_map/ppermute | solution.py:503
  28.2 0.0 collective-permute-done.4.strip_a
  28.2 0.0 collective-permute-done.2.raw_b
  28.2 0.0 collective-permute-done.3.raw_a
  28.2 11.2 %shard_map.85 = (f32[4536,128]{1,0:T(8,128)S(1)}, f32[1144,128]{1,0:T(8,128)S(1)}, f32[1760,128]{1,0:T(8,128)S(1)}, f32[1760,128]{1,0:T(8,128)S(1)}, f32[8,128]{...) custom-call(f32[3044,128]{1,0:T(8,128)S(1)} %pad_maximum_fusion.whole, f32[200,128]{1,0:T(8,128)S(1)} %shard_map.83.mine, ...), custom_call_target="tpu_custom_call" | custom-call | tf_op jit(solution)/shard_map/pallas_call | solution.py:57
  39.5 9.5 %all_to_all.5.got = f32[4,80,128]{2,1,0:T(8,128)S(1)} all-to-all(f32[4,80,128]{2,1,0:T(8,128)S(1)} %get-tuple-element.34), channel_id=1, replica_groups=mesh['tile'=128,'sub'=4] {'sub'}, dimensions={0} | all-to-all | bytes 327680 | tf_op jit(solution)/shard_map/all_to_all | solution.py:524
  49.0 0.0 copy-done
  49.0 0.0 copy-done.1
  49.0 0.0 copy-done.3
  49.0 0.5 shard_map.86
  49.5 3.0 %collective-permute-start.6 = (f32[40,128]{1,0:T(8,128)S(1)}, f32[40,128]{1,0:T(8,128)S(1)}, u32[]{:S(2)}, u32[]{:S(2)}) collective-permute-start(f32[40,128]{1,0:T(8,128)S(1)} %get-tuple-element.39), channel_id=1, source_target_pairs={{4,8},{12,16},{20,24},{28,32},{36,40},{44,48},{52,56},{60,64},{68,... | collective-permute-start | bytes 61448 | tf_op jit(solution)/shard_map/ppermute | solution.py:503
  52.6 1.9 %collective-permute-start.7 = (f32[40,128]{1,0:T(8,128)S(1)}, f32[40,128]{1,0:T(8,128)S(1)}, u32[]{:S(2)}, u32[]{:S(2)}) collective-permute-start(f32[40,128]{1,0:T(8,128)S(1)} %get-tuple-element.40), channel_id=1, source_target_pairs={{0,4},{8,12},{16,20},{24,28},{32,36},{40,44},{48,52},{56,60},{64,6... | collective-permute-start | bytes 61448 | tf_op jit(solution)/shard_map/ppermute | solution.py:503
  54.5 3.4 %collective-permute-done.6.got_b = f32[40,128]{1,0:T(8,128)S(1)} collective-permute-done((f32[40,128]{1,0:T(8,128)S(1)}, f32[40,128]{1,0:T(8,128)S(1)}, u32[]{:S(2)}, u32[]{:S(2)}) %collective-permute-start.6) | collective-permute-done | bytes 20512 | tf_op jit(solution)/shard_map/ppermute | solution.py:503
  58.0 0.0 collective-permute-done.7.got_a
  58.0 0.0 copy-done.2
  58.0 0.8 shard_map.87
  58.8 3.5 %collective-permute-start.8 = (f32[40,128]{1,0:T(8,128)S(1)}, f32[40,128]{1,0:T(8,128)S(1)}, u32[]{:S(2)}, u32[]{:S(2)}) collective-permute-start(f32[40,128]{1,0:T(8,128)S(1)} %get-tuple-element.42), channel_id=1, source_target_pairs={{4,8},{12,16},{20,24},{28,32},{36,40},{44,48},{52,56},{60,64},{68,... | collective-permute-start | bytes 61448 | tf_op jit(solution)/shard_map/ppermute | solution.py:503
  62.3 1.9 %collective-permute-start.9 = (f32[40,128]{1,0:T(8,128)S(1)}, f32[40,128]{1,0:T(8,128)S(1)}, u32[]{:S(2)}, u32[]{:S(2)}) collective-permute-start(f32[40,128]{1,0:T(8,128)S(1)} %get-tuple-element.43), channel_id=1, source_target_pairs={{0,4},{8,12},{16,20},{24,28},{32,36},{40,44},{48,52},{56,60},{64,6... | collective-permute-start | bytes 61448 | tf_op jit(solution)/shard_map/ppermute | solution.py:503
  64.2 2.9 %collective-permute-done.8.got_b = f32[40,128]{1,0:T(8,128)S(1)} collective-permute-done((f32[40,128]{1,0:T(8,128)S(1)}, f32[40,128]{1,0:T(8,128)S(1)}, u32[]{:S(2)}, u32[]{:S(2)}) %collective-permute-start.8) | collective-permute-done | bytes 20512 | tf_op jit(solution)/shard_map/ppermute | solution.py:503
  67.2 0.0 collective-permute-done.9.got_a
  67.2 0.8 shard_map.88
  68.0 3.5 %collective-permute-start.10 = (f32[40,128]{1,0:T(8,128)S(1)}, f32[40,128]{1,0:T(8,128)S(1)}, u32[]{:S(2)}, u32[]{:S(2)}) collective-permute-start(f32[40,128]{1,0:T(8,128)S(1)} %get-tuple-element.45), channel_id=1, source_target_pairs={{4,8},{12,16},{20,24},{28,32},{36,40},{44,48},{52,56},{60,64},{68,... | collective-permute-start | bytes 61448 | tf_op jit(solution)/shard_map/ppermute | solution.py:503
  71.5 1.9 %collective-permute-start.11 = (f32[40,128]{1,0:T(8,128)S(1)}, f32[40,128]{1,0:T(8,128)S(1)}, u32[]{:S(2)}, u32[]{:S(2)}) collective-permute-start(f32[40,128]{1,0:T(8,128)S(1)} %get-tuple-element.46), channel_id=1, source_target_pairs={{0,4},{8,12},{16,20},{24,28},{32,36},{40,44},{48,52},{56,60},{64,6... | collective-permute-start | bytes 61448 | tf_op jit(solution)/shard_map/ppermute | solution.py:503
  73.5 2.9 %collective-permute-done.10.got_b = f32[40,128]{1,0:T(8,128)S(1)} collective-permute-done((f32[40,128]{1,0:T(8,128)S(1)}, f32[40,128]{1,0:T(8,128)S(1)}, u32[]{:S(2)}, u32[]{:S(2)}) %collective-permute-start.10) | collective-permute-done | bytes 20512 | tf_op jit(solution)/shard_map/ppermute | solution.py:503
  76.4 0.0 collective-permute-done.11.got_a
  76.4 0.7 shard_map.89.level
  77.1 3.5 %collective-permute-start.13 = (f32[160,128]{1,0:T(8,128)S(1)}, f32[160,128]{1,0:T(8,128)S(1)}, u32[]{:S(2)}, u32[]{:S(2)}) collective-permute-start(f32[160,128]{1,0:T(8,128)S(1)} %shard_map.89.level), channel_id=1, source_target_pairs={{4,8},{12,16},{20,24},{28,32},{36,40},{44,48},{52,56},{60,64},{68,... | collective-permute-start | bytes 245768 | tf_op jit(solution)/shard_map/ppermute | solution.py:503
  80.6 1.9 %collective-permute-start.12 = (f32[160,128]{1,0:T(8,128)S(1)}, f32[160,128]{1,0:T(8,128)S(1)}, u32[]{:S(2)}, u32[]{:S(2)}) collective-permute-start(f32[160,128]{1,0:T(8,128)S(1)} %shard_map.89.level), channel_id=1, source_target_pairs={{0,4},{8,12},{16,20},{24,28},{32,36},{40,44},{48,52},{56,60},{64,6... | collective-permute-start | bytes 245768 | tf_op jit(solution)/shard_map/ppermute | solution.py:503
  82.6 3.6 %collective-permute-done.13.got_b = f32[160,128]{1,0:T(8,128)S(1)} collective-permute-done((f32[160,128]{1,0:T(8,128)S(1)}, f32[160,128]{1,0:T(8,128)S(1)}, u32[]{:S(2)}, u32[]{:S(2)}) %collective-permute-start.13) | collective-permute-done | bytes 81952 | tf_op jit(solution)/shard_map/ppermute | solution.py:503
  86.2 0.0 collective-permute-done.12.got_a
  86.2 7.2 %shard_map.90 = f32[640,128]{1,0:T(8,128)} custom-call(f32[4536,128]{1,0:T(8,128)S(1)} %get-tuple-element.28.coeffs_x, f32[1144,128]{1,0:T(8,128)S(1)} %get-tuple-element.29.inverse_x, f32[1760,128]{1,0:T(8,128)S(1)} %get-tuple-element.30.smoothed, f32[1760,128]{1,0:T(8,128)S(1)} %get-tuple-element.31.residual, f32[3044,128]{1,0:T(8,128)S(1)} %pad_maximum_fusion.whole, ...), custom_call_target="tpu_custom_call" | custom-call | tf_op jit(solution)/shard_map/pallas_call | solution.py:57
  (1 shorter events, 0.0 us)
Async XLA Ops:
  2.8 25.4 %collective-permute-start.2 = (f32[1808,128]{1,0:T(8,128)S(1)}, f32[1808,128]{1,0:T(8,128)S(1)}, u32[]{:S(2)}, u32[]{:S(2)}) collective-permute-start(f32[1808,128]{1,0:T(8,128)S(1)} %get-tuple-element.26), channel_id=1, source_target_pairs={{4,8},{12,16},{20,24},{28,32},{36,40},{44,48},{52,56},{60,64},{68,... | collective-permute-start | bytes 2777096 | tf_op jit(solution)/shard_map/ppermute | solution.py:503
  6.7 21.5 %collective-permute-start.3 = (f32[1808,128]{1,0:T(8,128)S(1)}, f32[1808,128]{1,0:T(8,128)S(1)}, u32[]{:S(2)}, u32[]{:S(2)}) collective-permute-start(f32[1808,128]{1,0:T(8,128)S(1)} %get-tuple-element.27), channel_id=1, source_target_pairs={{0,4},{8,12},{16,20},{24,28},{32,36},{40,44},{48,52},{56,60},{64,6... | collective-permute-start | bytes 2777096 | tf_op jit(solution)/shard_map/ppermute | solution.py:503
  8.6 6.8 %collective-permute-start.1 = (f32[200,128]{1,0:T(8,128)S(1)}, f32[200,128]{1,0:T(8,128)S(1)}, u32[]{:S(2)}, u32[]{:S(2)}) collective-permute-start(f32[200,128]{1,0:T(8,128)S(1)} %shard_map.82.packed), channel_id=1, source_target_pairs={{1,2},{2,1},{5,6},{6,5},{9,10},{10,9},{13,14},{14,13},{17,18},{18,... | collective-permute-start | bytes 307208 | tf_op jit(solution)/shard_map/ppermute | solution.py:513
  9.3 9.4 %collective-permute-start = (f32[200,128]{1,0:T(8,128)S(1)}, f32[200,128]{1,0:T(8,128)S(1)}, u32[]{:S(2)}, u32[]{:S(2)}) collective-permute-start(f32[200,128]{1,0:T(8,128)S(1)} %shard_map.82.packed), channel_id=1, source_target_pairs={{0,1},{2,3},{1,0},{3,2},{4,5},{6,7},{5,4},{7,6},{8,9},{10,11},{9,8... | collective-permute-start | bytes 307208 | tf_op jit(solution)/shard_map/ppermute | solution.py:512
  18.7 30.3 %copy-start = (f32[5,10,10,256]{3,2,1,0:T(8,128)S(1)}, f32[5,10,10,256]{3,2,1,0:T(8,128)}, u32[]{:S(2)}) copy-start(f32[5,10,10,256]{3,2,1,0:T(8,128)} %coeffs.1) | copy-start | bytes 1536004
  18.7 30.3 %copy-start.1 = (f32[10,10,256]{2,1,0:T(8,128)S(1)}, f32[10,10,256]{2,1,0:T(8,128)}, u32[]{:S(2)}) copy-start(f32[10,10,256]{2,1,0:T(8,128)} %inverse.1) | copy-start | bytes 307204
  18.7 30.3 %copy-start.3 = (s32[2,32]{1,0:T(2,128)S(1)}, s32[2,32]{1,0:T(2,128)}, u32[]{:S(2)}) copy-start(s32[2,32]{1,0:T(2,128)} %send.5) | copy-start | bytes 772
  18.8 39.2 %copy-start.2 = (s32[5,256]{1,0:T(8,128)S(1)}, s32[5,256]{1,0:T(8,128)}, u32[]{:S(2)}) copy-start(s32[5,256]{1,0:T(8,128)} %cols.5) | copy-start | bytes 15364
  18.8 9.4 %collective-permute-start.5 = (f32[200,128]{1,0:T(8,128)S(1)}, f32[200,128]{1,0:T(8,128)S(1)}, u32[]{:S(2)}, u32[]{:S(2)}) collective-permute-start(f32[200,128]{1,0:T(8,128)S(1)} %shard_map.83.mine), channel_id=1, source_target_pairs={{4,8},{12,16},{20,24},{28,32},{36,40},{44,48},{52,56},{60,64},{68,... | collective-permute-start | bytes 307208 | tf_op jit(solution)/shard_map/ppermute | solution.py:503
  22.5 5.7 %collective-permute-start.4 = (f32[200,128]{1,0:T(8,128)S(1)}, f32[200,128]{1,0:T(8,128)S(1)}, u32[]{:S(2)}, u32[]{:S(2)}) collective-permute-start(f32[200,128]{1,0:T(8,128)S(1)} %shard_map.83.mine), channel_id=1, source_target_pairs={{0,4},{8,12},{16,20},{24,28},{32,36},{40,44},{48,52},{56,60},{64,6... | collective-permute-start | bytes 307208 | tf_op jit(solution)/shard_map/ppermute | solution.py:503
  49.5 8.4 %collective-permute-start.6 = (f32[40,128]{1,0:T(8,128)S(1)}, f32[40,128]{1,0:T(8,128)S(1)}, u32[]{:S(2)}, u32[]{:S(2)}) collective-permute-start(f32[40,128]{1,0:T(8,128)S(1)} %get-tuple-element.39), channel_id=1, source_target_pairs={{4,8},{12,16},{20,24},{28,32},{36,40},{44,48},{52,56},{60,64},{68,... | collective-permute-start | bytes 61448 | tf_op jit(solution)/shard_map/ppermute | solution.py:503
  52.6 5.4 %collective-permute-start.7 = (f32[40,128]{1,0:T(8,128)S(1)}, f32[40,128]{1,0:T(8,128)S(1)}, u32[]{:S(2)}, u32[]{:S(2)}) collective-permute-start(f32[40,128]{1,0:T(8,128)S(1)} %get-tuple-element.40), channel_id=1, source_target_pairs={{0,4},{8,12},{16,20},{24,28},{32,36},{40,44},{48,52},{56,60},{64,6... | collective-permute-start | bytes 61448 | tf_op jit(solution)/shard_map/ppermute | solution.py:503
  58.8 8.4 %collective-permute-start.8 = (f32[40,128]{1,0:T(8,128)S(1)}, f32[40,128]{1,0:T(8,128)S(1)}, u32[]{:S(2)}, u32[]{:S(2)}) collective-permute-start(f32[40,128]{1,0:T(8,128)S(1)} %get-tuple-element.42), channel_id=1, source_target_pairs={{4,8},{12,16},{20,24},{28,32},{36,40},{44,48},{52,56},{60,64},{68,... | collective-permute-start | bytes 61448 | tf_op jit(solution)/shard_map/ppermute | solution.py:503
  62.3 4.9 %collective-permute-start.9 = (f32[40,128]{1,0:T(8,128)S(1)}, f32[40,128]{1,0:T(8,128)S(1)}, u32[]{:S(2)}, u32[]{:S(2)}) collective-permute-start(f32[40,128]{1,0:T(8,128)S(1)} %get-tuple-element.43), channel_id=1, source_target_pairs={{0,4},{8,12},{16,20},{24,28},{32,36},{40,44},{48,52},{56,60},{64,6... | collective-permute-start | bytes 61448 | tf_op jit(solution)/shard_map/ppermute | solution.py:503
  68.0 8.4 %collective-permute-start.10 = (f32[40,128]{1,0:T(8,128)S(1)}, f32[40,128]{1,0:T(8,128)S(1)}, u32[]{:S(2)}, u32[]{:S(2)}) collective-permute-start(f32[40,128]{1,0:T(8,128)S(1)} %get-tuple-element.45), channel_id=1, source_target_pairs={{4,8},{12,16},{20,24},{28,32},{36,40},{44,48},{52,56},{60,64},{68,... | collective-permute-start | bytes 61448 | tf_op jit(solution)/shard_map/ppermute | solution.py:503
  71.5 4.9 %collective-permute-start.11 = (f32[40,128]{1,0:T(8,128)S(1)}, f32[40,128]{1,0:T(8,128)S(1)}, u32[]{:S(2)}, u32[]{:S(2)}) collective-permute-start(f32[40,128]{1,0:T(8,128)S(1)} %get-tuple-element.46), channel_id=1, source_target_pairs={{0,4},{8,12},{16,20},{24,28},{32,36},{40,44},{48,52},{56,60},{64,6... | collective-permute-start | bytes 61448 | tf_op jit(solution)/shard_map/ppermute | solution.py:503
  77.1 9.1 %collective-permute-start.13 = (f32[160,128]{1,0:T(8,128)S(1)}, f32[160,128]{1,0:T(8,128)S(1)}, u32[]{:S(2)}, u32[]{:S(2)}) collective-permute-start(f32[160,128]{1,0:T(8,128)S(1)} %shard_map.89.level), channel_id=1, source_target_pairs={{4,8},{12,16},{20,24},{28,32},{36,40},{44,48},{52,56},{60,64},{68,... | collective-permute-start | bytes 245768 | tf_op jit(solution)/shard_map/ppermute | solution.py:503
  80.6 5.5 %collective-permute-start.12 = (f32[160,128]{1,0:T(8,128)S(1)}, f32[160,128]{1,0:T(8,128)S(1)}, u32[]{:S(2)}, u32[]{:S(2)}) collective-permute-start(f32[160,128]{1,0:T(8,128)S(1)} %shard_map.89.level), channel_id=1, source_target_pairs={{0,4},{8,12},{16,20},{24,28},{32,36},{40,44},{48,52},{56,60},{64,6... | collective-permute-start | bytes 245768 | tf_op jit(solution)/shard_map/ppermute | solution.py:503

commit v3 on v2

--- a/solution.py
+++ b/solution.py
@@ -99,7 +99,7 @@
     second = jnp.where(at_row == 0, aggregate[pl.ds(1, 1), :], aggregate[pl.ds(3, 1), :])
     sublane = lax.broadcasted_iota(I32, (8, 128), 0)
     both = jnp.where(sublane == 0, jnp.broadcast_to(first, (8, 128)), jnp.broadcast_to(second, (8, 128)))
-    out[pl.ds(RAW_G, 8), :] = both
+    out[pl.ds(RAW_G, 8), :] = both.astype(F32)
 
 
 class Rows:
@@ -112,11 +112,11 @@
 
 
 def parts(whole):
-    return [Rows(whole, first) for first in (0, 640, 1040, 3040)]
-
-
-def pack_kernel(whole, packed_out):
-    rhs, inverse, coeffs, aggregate = parts(whole)
+    return [Rows(whole, first) for first in (0, 640, 1040)]
+
+
+def pack_kernel(whole, aggregate, packed_out):
+    rhs, inverse, coeffs = parts(whole)
     lane = lanes()
     index = slot_columns(lane)
     window = lane >> 3
@@ -126,15 +126,15 @@
         for k, (kind, start) in enumerate(GROUPS[4 * q : 4 * q + 4]):
             for x in range(4):
                 if kind == "g":
-                    block = jnp.broadcast_to(aggregate[pl.ds(x, 1), :], (8, 128))
+                    block = jnp.broadcast_to(aggregate[pl.ds(x, 1), :].astype(F32), (8, 128))
                 else:
                     block = sources[kind][pl.ds(4 * start + x, 8, stride=4), :]
                 packed = jnp.where(window == 4 * k + x, pick(block, index), packed)
         packed_out[pl.ds(8 * q, 8), :] = packed
 
 
-def raw_kernel(packed, whole, raw_b, raw_a):
-    rhs, inverse, coeffs, aggregate = parts(whole)
+def raw_kernel(packed, whole, aggregate, raw_b, raw_a):
+    rhs, inverse, coeffs = parts(whole)
     odd = odd_tile()
     raw_message(raw_b, odd, rhs, inverse, coeffs, aggregate)
     raw_message(raw_a, 1 - odd, rhs, inverse, coeffs, aggregate)
@@ -236,13 +236,13 @@
 
 
 def down_kernel(
-    whole, mine, raw_b, raw_a, strip_a, strip_b,
+    whole, aggregate, mine, raw_b, raw_a, strip_a, strip_b,
     coeffs_x, inverse_x, smoothed, residual, index_s, index_t, out,
     rhs_x, first, scaled, filtered, moved,
 ):
     lane = lanes()
     slot = lane & 7
-    rhs, inverse, coeffs, aggregate = parts(whole)
+    rhs, inverse, coeffs = parts(whole)
     odd = odd_tile() == 1
     needed = (lane >= 8) & (lane < 72) & ((slot == 1) | (slot == 2) | (slot == 5) | (slot == 6))
     for q in range(PACKED // 8):
@@ -325,7 +325,7 @@
     member = lax.broadcasted_iota(I32, (128, 128), 0) & 63
     summed = jnp.zeros((FC, 128), F32)
     for x in range(4):
-        owner = jnp.broadcast_to(aggregate[pl.ds(x, 1), :].astype(I32), (128, 128))
+        owner = jnp.broadcast_to(aggregate[pl.ds(x, 1), :], (128, 128))
         table = (owner == member).astype(F32).astype(jnp.bfloat16)
         rest = filtered[pl.ds(x * FC, FC), :]
         for _ in range(3):
@@ -425,7 +425,7 @@
 
 
 def up_kernel(
-    coeffs_x, inverse_x, smoothed, residual, whole, index_s, index_t, level, got_a, got_b,
+    coeffs_x, inverse_x, smoothed, residual, aggregate, index_s, index_t, level, got_a, got_b,
     out, spread, applied, scaled, moved,
 ):
     lane = lanes()
@@ -437,8 +437,7 @@
         return jnp.where(s <= 0, 0, jnp.where(s == 1, 64, jnp.where(s == 2, 96, 112)))
 
     own_at = offset(sub)
-    aggregate = parts(whole)[3]
-    mains = [jnp.minimum(row(aggregate, x).astype(I32) + own_at, 127) for x in range(4)]
+    mains = [jnp.minimum(row(aggregate, x) + own_at, 127) for x in range(4)]
     outers = [jnp.minimum(spread_row(index_t, r).astype(I32) + own_at, 127) for r in range(4)]
     side = jnp.where(slot <= 2, offset(sub + 1), offset(sub - 1))
     beside = jnp.minimum(index_s[...].astype(I32) + side, 127)
@@ -507,18 +506,18 @@
     coeffs = fine_coeffs.reshape(2000, 128)
     slabs, small, cvec = (SLABS * FC, 128), (40, 128), (FC, 128)
 
-    whole = jnp.concatenate([rhs, inverse, coeffs, aggregate.astype(F32)], axis=0)
-    (packed,) = call(pack_kernel, [(PACKED, 128)], [whole])
+    whole = jnp.concatenate([rhs, inverse, coeffs], axis=0)
+    (packed,) = call(pack_kernel, [(PACKED, 128)], [whole, aggregate])
     got_1 = lax.ppermute(packed, "sub", sub_1)
     got_2 = lax.ppermute(packed, "sub", sub_2)
-    raw_b, raw_a = call(raw_kernel, [(RAW, 128), (RAW, 128)], [packed, whole])
+    raw_b, raw_a = call(raw_kernel, [(RAW, 128), (RAW, 128)], [packed, whole, aggregate])
     raw = trade(raw_b, raw_a)
     (mine,) = call(merge_kernel, [(PACKED, 128)], [got_1, got_2])
     strips = trade(mine, mine)[::-1]
     coeffs_x, inverse_x, smoothed, residual, index_s, index_t, summed = call(
         down_kernel,
         [(9 * NIJ, 128), (SLABS * IJ, 128), slabs, slabs, (8, 128), (8, 128), (4, 80, 128)],
-        [whole, mine, *raw, *strips],
+        [whole, aggregate, mine, *raw, *strips],
         [slabs, slabs, slabs, (4 * FC, 128), (4 * FC, 128)],
     )
     summed = lax.all_to_all(summed, "sub", 0, 0)
@@ -541,7 +540,7 @@
     (out,) = call(
         up_kernel,
         [(640, 128)],
-        [coeffs_x, inverse_x, smoothed, residual, whole, index_s, index_t, level, *trade(level, level)[::-1]],
+        [coeffs_x, inverse_x, smoothed, residual, aggregate, index_s, index_t, level, *trade(level, level)[::-1]],
         [slabs, slabs, slabs, (4 * FC, 128)],
     )
     return out.reshape(right_side.shape)

time: 93.9 us -> 93.2 us (level)
  no operation moved by 1% of the time
where the time goes in v3:
time: 93.2 us; the launch traced here: 92.7 us
  starting transfers between devices  39.7 us (43%)
  Pallas kernels  21.9 us (23%)
  waiting for transfers between devices  19.9 us (21%)
  blocking collectives  9.53 us (10%)
  other arithmetic  1.46 us (2%)
    pallas_call x9, Pallas kernels, call(): pl.pallas_call(kernel, out_shape=[shape(s) for s in outs], in_specs=specs...  21.9 us
    ppermute x6, starting transfers between devices, trade(): lax.ppermute(to_b, 'tile', tile_b)  21.4 us
    ppermute x6, waiting for transfers between devices, trade(): lax.ppermute(to_b, 'tile', tile_b)  16.6 us
    ppermute x6, starting transfers between devices, trade(): lax.ppermute(to_a, 'tile', tile_a)  11.5 us
    all_to_all x1, blocking collectives, body(): summed = lax.all_to_all(summed, 'sub', 0, 0)  9.53 us
    ppermute x1, starting transfers between devices, body(): got_1 = lax.ppermute(packed, 'sub', sub_1)  6.13 us
    ppermute x1, waiting for transfers between devices, body(): got_1 = lax.ppermute(packed, 'sub', sub_1)  3.24 us
  transfers between devices with their start and end apart: 14, of which 6 were waited for; matrix products, arithmetic and copies ran while one was open for 0% of the time, Pallas kernels for 0%

profile of v3, /device:TPU:256, one launch (start us, length us, event | category | flops | bytes accessed | tf_op | source)
XLA Modules:
  0.0 92.7 jit_solution(9539169611820913986)
XLA Ops:
  0.0 0.0 copy-start.3
  0.0 1.5 %pad_maximum_fusion.whole = f32[3040,128]{1,0:T(8,128)S(1)} fusion(f32[2000,128]{1,0:T(8,128)} %bitcast.4, f32[400,128]{1,0:T(8,128)} %bitcast.6, f32[640,128]{1,0:T(8,128)} %bitcast.5), kind=kLoop, calls=%fused_computation | loop fusion | flops 778240 | bytes 3112960 | tf_op jit(solution)/shard_map/concatenate | solution.py:509
  1.5 0.0 copy-done.3
  1.5 0.5 shard_map.82.packed
  2.0 0.2 shard_map.84
  2.1 3.9 %collective-permute-start.2 = (f32[1808,128]{1,0:T(8,128)S(1)}, f32[1808,128]{1,0:T(8,128)S(1)}, u32[]{:S(2)}, u32[]{:S(2)}) collective-permute-start(f32[1808,128]{1,0:T(8,128)S(1)} %get-tuple-element.26), channel_id=1, source_target_pairs={{4,8},{12,16},{20,24},{28,32},{36,40},{44,48},{52,56},{60,64},{68,... | collective-permute-start | bytes 2777096 | tf_op jit(solution)/shard_map/ppermute | solution.py:502
  6.0 1.9 %collective-permute-start.3 = (f32[1808,128]{1,0:T(8,128)S(1)}, f32[1808,128]{1,0:T(8,128)S(1)}, u32[]{:S(2)}, u32[]{:S(2)}) collective-permute-start(f32[1808,128]{1,0:T(8,128)S(1)} %get-tuple-element.27), channel_id=1, source_target_pairs={{0,4},{8,12},{16,20},{24,28},{32,36},{40,44},{48,52},{56,60},{64,6... | collective-permute-start | bytes 2777096 | tf_op jit(solution)/shard_map/ppermute | solution.py:502
  8.0 0.7 collective-permute-start.1
  8.7 6.1 %collective-permute-start = (f32[200,128]{1,0:T(8,128)S(1)}, f32[200,128]{1,0:T(8,128)S(1)}, u32[]{:S(2)}, u32[]{:S(2)}) collective-permute-start(f32[200,128]{1,0:T(8,128)S(1)} %shard_map.82.packed), channel_id=1, source_target_pairs={{0,1},{2,3},{1,0},{3,2},{4,5},{6,7},{5,4},{7,6},{8,9},{10,11},{9,8... | collective-permute-start | bytes 307208 | tf_op jit(solution)/shard_map/ppermute | solution.py:511
  14.8 0.0 collective-permute-done.1.got_2
  14.8 3.2 %collective-permute-done.got_1 = f32[200,128]{1,0:T(8,128)S(1)} collective-permute-done((f32[200,128]{1,0:T(8,128)S(1)}, f32[200,128]{1,0:T(8,128)S(1)}, u32[]{:S(2)}, u32[]{:S(2)}) %collective-permute-start) | collective-permute-done | bytes 102432 | tf_op jit(solution)/shard_map/ppermute | solution.py:511
  18.1 0.0 copy-start
  18.1 0.0 copy-start.1
  18.1 0.0 copy-start.4
  18.1 0.0 copy-start.2
  18.1 3.8 %collective-permute-start.5 = (f32[200,128]{1,0:T(8,128)S(1)}, f32[200,128]{1,0:T(8,128)S(1)}, u32[]{:S(2)}, u32[]{:S(2)}) collective-permute-start(f32[200,128]{1,0:T(8,128)S(1)} %shard_map.83.mine), channel_id=1, source_target_pairs={{4,8},{12,16},{20,24},{28,32},{36,40},{44,48},{52,56},{60,64},{68,... | collective-permute-start | bytes 307208 | tf_op jit(solution)/shard_map/ppermute | solution.py:502
  21.9 1.9 %collective-permute-start.4 = (f32[200,128]{1,0:T(8,128)S(1)}, f32[200,128]{1,0:T(8,128)S(1)}, u32[]{:S(2)}, u32[]{:S(2)}) collective-permute-start(f32[200,128]{1,0:T(8,128)S(1)} %shard_map.83.mine), channel_id=1, source_target_pairs={{0,4},{8,12},{16,20},{24,28},{32,36},{40,44},{48,52},{56,60},{64,6... | collective-permute-start | bytes 307208 | tf_op jit(solution)/shard_map/ppermute | solution.py:502
  23.8 3.7 %collective-permute-done.5.strip_b = f32[200,128]{1,0:T(8,128)S(1)} collective-permute-done((f32[200,128]{1,0:T(8,128)S(1)}, f32[200,128]{1,0:T(8,128)S(1)}, u32[]{:S(2)}, u32[]{:S(2)}) %collective-permute-start.5) | collective-permute-done | bytes 102432 | tf_op jit(solution)/shard_map/ppermute | solution.py:502
  27.5 0.0 collective-permute-done.4.strip_a
  27.5 0.0 collective-permute-done.2.raw_b
  27.6 0.0 collective-permute-done.3.raw_a
  27.6 11.2 %shard_map.85 = (f32[4536,128]{1,0:T(8,128)S(1)}, f32[1144,128]{1,0:T(8,128)S(1)}, f32[1760,128]{1,0:T(8,128)S(1)}, f32[1760,128]{1,0:T(8,128)S(1)}, f32[8,128]{...) custom-call(f32[3040,128]{1,0:T(8,128)S(1)} %pad_maximum_fusion.whole, s32[4,128]{1,0:T(4,128)S(1)} %copy-done.3, ...), custom_call_target="tpu_custom_call" | custom-call | tf_op jit(solution)/shard_map/pallas_call | solution.py:57
  38.8 9.5 %all_to_all.5.got = f32[4,80,128]{2,1,0:T(8,128)S(1)} all-to-all(f32[4,80,128]{2,1,0:T(8,128)S(1)} %get-tuple-element.34), channel_id=1, replica_groups=mesh['tile'=128,'sub'=4] {'sub'}, dimensions={0} | all-to-all | bytes 327680 | tf_op jit(solution)/shard_map/all_to_all | solution.py:523
  48.3 0.0 copy-done
  48.3 0.0 copy-done.1
  48.3 0.0 copy-done.4
  48.3 0.5 shard_map.86
  48.8 3.0 %collective-permute-start.6 = (f32[40,128]{1,0:T(8,128)S(1)}, f32[40,128]{1,0:T(8,128)S(1)}, u32[]{:S(2)}, u32[]{:S(2)}) collective-permute-start(f32[40,128]{1,0:T(8,128)S(1)} %get-tuple-element.39), channel_id=1, source_target_pairs={{4,8},{12,16},{20,24},{28,32},{36,40},{44,48},{52,56},{60,64},{68,... | collective-permute-start | bytes 61448 | tf_op jit(solution)/shard_map/ppermute | solution.py:502
  51.9 1.9 %collective-permute-start.7 = (f32[40,128]{1,0:T(8,128)S(1)}, f32[40,128]{1,0:T(8,128)S(1)}, u32[]{:S(2)}, u32[]{:S(2)}) collective-permute-start(f32[40,128]{1,0:T(8,128)S(1)} %get-tuple-element.40), channel_id=1, source_target_pairs={{0,4},{8,12},{16,20},{24,28},{32,36},{40,44},{48,52},{56,60},{64,6... | collective-permute-start | bytes 61448 | tf_op jit(solution)/shard_map/ppermute | solution.py:502
  53.8 3.4 %collective-permute-done.6.got_b = f32[40,128]{1,0:T(8,128)S(1)} collective-permute-done((f32[40,128]{1,0:T(8,128)S(1)}, f32[40,128]{1,0:T(8,128)S(1)}, u32[]{:S(2)}, u32[]{:S(2)}) %collective-permute-start.6) | collective-permute-done | bytes 20512 | tf_op jit(solution)/shard_map/ppermute | solution.py:502
  57.3 0.0 collective-permute-done.7.got_a
  57.3 0.0 copy-done.2
  57.3 0.8 shard_map.87
  58.1 3.5 %collective-permute-start.8 = (f32[40,128]{1,0:T(8,128)S(1)}, f32[40,128]{1,0:T(8,128)S(1)}, u32[]{:S(2)}, u32[]{:S(2)}) collective-permute-start(f32[40,128]{1,0:T(8,128)S(1)} %get-tuple-element.42), channel_id=1, source_target_pairs={{4,8},{12,16},{20,24},{28,32},{36,40},{44,48},{52,56},{60,64},{68,... | collective-permute-start | bytes 61448 | tf_op jit(solution)/shard_map/ppermute | solution.py:502
  61.6 1.9 %collective-permute-start.9 = (f32[40,128]{1,0:T(8,128)S(1)}, f32[40,128]{1,0:T(8,128)S(1)}, u32[]{:S(2)}, u32[]{:S(2)}) collective-permute-start(f32[40,128]{1,0:T(8,128)S(1)} %get-tuple-element.43), channel_id=1, source_target_pairs={{0,4},{8,12},{16,20},{24,28},{32,36},{40,44},{48,52},{56,60},{64,6... | collective-permute-start | bytes 61448 | tf_op jit(solution)/shard_map/ppermute | solution.py:502
  63.5 2.9 %collective-permute-done.8.got_b = f32[40,128]{1,0:T(8,128)S(1)} collective-permute-done((f32[40,128]{1,0:T(8,128)S(1)}, f32[40,128]{1,0:T(8,128)S(1)}, u32[]{:S(2)}, u32[]{:S(2)}) %collective-permute-start.8) | collective-permute-done | bytes 20512 | tf_op jit(solution)/shard_map/ppermute | solution.py:502
  66.5 0.0 collective-permute-done.9.got_a
  66.5 0.8 shard_map.88
  67.3 3.5 %collective-permute-start.10 = (f32[40,128]{1,0:T(8,128)S(1)}, f32[40,128]{1,0:T(8,128)S(1)}, u32[]{:S(2)}, u32[]{:S(2)}) collective-permute-start(f32[40,128]{1,0:T(8,128)S(1)} %get-tuple-element.45), channel_id=1, source_target_pairs={{4,8},{12,16},{20,24},{28,32},{36,40},{44,48},{52,56},{60,64},{68,... | collective-permute-start | bytes 61448 | tf_op jit(solution)/shard_map/ppermute | solution.py:502
  70.8 1.9 %collective-permute-start.11 = (f32[40,128]{1,0:T(8,128)S(1)}, f32[40,128]{1,0:T(8,128)S(1)}, u32[]{:S(2)}, u32[]{:S(2)}) collective-permute-start(f32[40,128]{1,0:T(8,128)S(1)} %get-tuple-element.46), channel_id=1, source_target_pairs={{0,4},{8,12},{16,20},{24,28},{32,36},{40,44},{48,52},{56,60},{64,6... | collective-permute-start | bytes 61448 | tf_op jit(solution)/shard_map/ppermute | solution.py:502
  72.8 2.9 %collective-permute-done.10.got_b = f32[40,128]{1,0:T(8,128)S(1)} collective-permute-done((f32[40,128]{1,0:T(8,128)S(1)}, f32[40,128]{1,0:T(8,128)S(1)}, u32[]{:S(2)}, u32[]{:S(2)}) %collective-permute-start.10) | collective-permute-done | bytes 20512 | tf_op jit(solution)/shard_map/ppermute | solution.py:502
  75.7 0.0 collective-permute-done.11.got_a
  75.7 0.7 shard_map.89.level
  76.4 3.5 %collective-permute-start.13 = (f32[160,128]{1,0:T(8,128)S(1)}, f32[160,128]{1,0:T(8,128)S(1)}, u32[]{:S(2)}, u32[]{:S(2)}) collective-permute-start(f32[160,128]{1,0:T(8,128)S(1)} %shard_map.89.level), channel_id=1, source_target_pairs={{4,8},{12,16},{20,24},{28,32},{36,40},{44,48},{52,56},{60,64},{68,... | collective-permute-start | bytes 245768 | tf_op jit(solution)/shard_map/ppermute | solution.py:502
  79.9 1.9 %collective-permute-start.12 = (f32[160,128]{1,0:T(8,128)S(1)}, f32[160,128]{1,0:T(8,128)S(1)}, u32[]{:S(2)}, u32[]{:S(2)}) collective-permute-start(f32[160,128]{1,0:T(8,128)S(1)} %shard_map.89.level), channel_id=1, source_target_pairs={{0,4},{8,12},{16,20},{24,28},{32,36},{40,44},{48,52},{56,60},{64,6... | collective-permute-start | bytes 245768 | tf_op jit(solution)/shard_map/ppermute | solution.py:502
  81.9 3.6 %collective-permute-done.13.got_b = f32[160,128]{1,0:T(8,128)S(1)} collective-permute-done((f32[160,128]{1,0:T(8,128)S(1)}, f32[160,128]{1,0:T(8,128)S(1)}, u32[]{:S(2)}, u32[]{:S(2)}) %collective-permute-start.13) | collective-permute-done | bytes 81952 | tf_op jit(solution)/shard_map/ppermute | solution.py:502
  85.5 0.0 collective-permute-done.12.got_a
  85.5 7.2 %shard_map.90 = f32[640,128]{1,0:T(8,128)} custom-call(f32[4536,128]{1,0:T(8,128)S(1)} %get-tuple-element.28.coeffs_x, f32[1144,128]{1,0:T(8,128)S(1)} %get-tuple-element.29.inverse_x, f32[1760,128]{1,0:T(8,128)S(1)} %get-tuple-element.30.smoothed, f32[1760,128]{1,0:T(8,128)S(1)} %get-tuple-element.31.residual, s32[4,128]{1,0:T(4,128)S(1)} %copy-done.3, ...), custom_call_target="tpu_custom_call" | custom-call | tf_op jit(solution)/shard_map/pallas_call | solution.py:57
  (1 shorter events, 0.0 us)
Async XLA Ops:
  0.0 1.5 %copy-start.3 = (s32[4,128]{1,0:T(4,128)S(1)}, s32[4,128]{1,0:T(4,128)}, u32[]{:S(2)}) copy-start(s32[4,128]{1,0:T(4,128)} %aggregate.7) | copy-start | bytes 6148
  2.1 25.4 %collective-permute-start.2 = (f32[1808,128]{1,0:T(8,128)S(1)}, f32[1808,128]{1,0:T(8,128)S(1)}, u32[]{:S(2)}, u32[]{:S(2)}) collective-permute-start(f32[1808,128]{1,0:T(8,128)S(1)} %get-tuple-element.26), channel_id=1, source_target_pairs={{4,8},{12,16},{20,24},{28,32},{36,40},{44,48},{52,56},{60,64},{68,... | collective-permute-start | bytes 2777096 | tf_op jit(solution)/shard_map/ppermute | solution.py:502
  6.0 21.5 %collective-permute-start.3 = (f32[1808,128]{1,0:T(8,128)S(1)}, f32[1808,128]{1,0:T(8,128)S(1)}, u32[]{:S(2)}, u32[]{:S(2)}) collective-permute-start(f32[1808,128]{1,0:T(8,128)S(1)} %get-tuple-element.27), channel_id=1, source_target_pairs={{0,4},{8,12},{16,20},{24,28},{32,36},{40,44},{48,52},{56,60},{64,6... | collective-permute-start | bytes 2777096 | tf_op jit(solution)/shard_map/ppermute | solution.py:502
  8.0 6.8 %collective-permute-start.1 = (f32[200,128]{1,0:T(8,128)S(1)}, f32[200,128]{1,0:T(8,128)S(1)}, u32[]{:S(2)}, u32[]{:S(2)}) collective-permute-start(f32[200,128]{1,0:T(8,128)S(1)} %shard_map.82.packed), channel_id=1, source_target_pairs={{1,2},{2,1},{5,6},{6,5},{9,10},{10,9},{13,14},{14,13},{17,18},{18,... | collective-permute-start | bytes 307208 | tf_op jit(solution)/shard_map/ppermute | solution.py:512
  8.7 9.4 %collective-permute-start = (f32[200,128]{1,0:T(8,128)S(1)}, f32[200,128]{1,0:T(8,128)S(1)}, u32[]{:S(2)}, u32[]{:S(2)}) collective-permute-start(f32[200,128]{1,0:T(8,128)S(1)} %shard_map.82.packed), channel_id=1, source_target_pairs={{0,1},{2,3},{1,0},{3,2},{4,5},{6,7},{5,4},{7,6},{8,9},{10,11},{9,8... | collective-permute-start | bytes 307208 | tf_op jit(solution)/shard_map/ppermute | solution.py:511
  18.1 30.2 %copy-start = (f32[5,10,10,256]{3,2,1,0:T(8,128)S(1)}, f32[5,10,10,256]{3,2,1,0:T(8,128)}, u32[]{:S(2)}) copy-start(f32[5,10,10,256]{3,2,1,0:T(8,128)} %coeffs.1) | copy-start | bytes 1536004
  18.1 30.2 %copy-start.1 = (f32[10,10,256]{2,1,0:T(8,128)S(1)}, f32[10,10,256]{2,1,0:T(8,128)}, u32[]{:S(2)}) copy-start(f32[10,10,256]{2,1,0:T(8,128)} %inverse.1) | copy-start | bytes 307204
  18.1 30.2 %copy-start.4 = (s32[2,32]{1,0:T(2,128)S(1)}, s32[2,32]{1,0:T(2,128)}, u32[]{:S(2)}) copy-start(s32[2,32]{1,0:T(2,128)} %send.5) | copy-start | bytes 772
  18.1 39.2 %copy-start.2 = (s32[5,256]{1,0:T(8,128)S(1)}, s32[5,256]{1,0:T(8,128)}, u32[]{:S(2)}) copy-start(s32[5,256]{1,0:T(8,128)} %cols.5) | copy-start | bytes 15364
  18.1 9.4 %collective-permute-start.5 = (f32[200,128]{1,0:T(8,128)S(1)}, f32[200,128]{1,0:T(8,128)S(1)}, u32[]{:S(2)}, u32[]{:S(2)}) collective-permute-start(f32[200,128]{1,0:T(8,128)S(1)} %shard_map.83.mine), channel_id=1, source_target_pairs={{4,8},{12,16},{20,24},{28,32},{36,40},{44,48},{52,56},{60,64},{68,... | collective-permute-start | bytes 307208 | tf_op jit(solution)/shard_map/ppermute | solution.py:502
  21.9 5.7 %collective-permute-start.4 = (f32[200,128]{1,0:T(8,128)S(1)}, f32[200,128]{1,0:T(8,128)S(1)}, u32[]{:S(2)}, u32[]{:S(2)}) collective-permute-start(f32[200,128]{1,0:T(8,128)S(1)} %shard_map.83.mine), channel_id=1, source_target_pairs={{0,4},{8,12},{16,20},{24,28},{32,36},{40,44},{48,52},{56,60},{64,6... | collective-permute-start | bytes 307208 | tf_op jit(solution)/shard_map/ppermute | solution.py:502
  48.8 8.4 %collective-permute-start.6 = (f32[40,128]{1,0:T(8,128)S(1)}, f32[40,128]{1,0:T(8,128)S(1)}, u32[]{:S(2)}, u32[]{:S(2)}) collective-permute-start(f32[40,128]{1,0:T(8,128)S(1)} %get-tuple-element.39), channel_id=1, source_target_pairs={{4,8},{12,16},{20,24},{28,32},{36,40},{44,48},{52,56},{60,64},{68,... | collective-permute-start | bytes 61448 | tf_op jit(solution)/shard_map/ppermute | solution.py:502
  51.9 5.4 %collective-permute-start.7 = (f32[40,128]{1,0:T(8,128)S(1)}, f32[40,128]{1,0:T(8,128)S(1)}, u32[]{:S(2)}, u32[]{:S(2)}) collective-permute-start(f32[40,128]{1,0:T(8,128)S(1)} %get-tuple-element.40), channel_id=1, source_target_pairs={{0,4},{8,12},{16,20},{24,28},{32,36},{40,44},{48,52},{56,60},{64,6... | collective-permute-start | bytes 61448 | tf_op jit(solution)/shard_map/ppermute | solution.py:502
  58.1 8.4 %collective-permute-start.8 = (f32[40,128]{1,0:T(8,128)S(1)}, f32[40,128]{1,0:T(8,128)S(1)}, u32[]{:S(2)}, u32[]{:S(2)}) collective-permute-start(f32[40,128]{1,0:T(8,128)S(1)} %get-tuple-element.42), channel_id=1, source_target_pairs={{4,8},{12,16},{20,24},{28,32},{36,40},{44,48},{52,56},{60,64},{68,... | collective-permute-start | bytes 61448 | tf_op jit(solution)/shard_map/ppermute | solution.py:502
  61.6 4.9 %collective-permute-start.9 = (f32[40,128]{1,0:T(8,128)S(1)}, f32[40,128]{1,0:T(8,128)S(1)}, u32[]{:S(2)}, u32[]{:S(2)}) collective-permute-start(f32[40,128]{1,0:T(8,128)S(1)} %get-tuple-element.43), channel_id=1, source_target_pairs={{0,4},{8,12},{16,20},{24,28},{32,36},{40,44},{48,52},{56,60},{64,6... | collective-permute-start | bytes 61448 | tf_op jit(solution)/shard_map/ppermute | solution.py:502
  67.3 8.4 %collective-permute-start.10 = (f32[40,128]{1,0:T(8,128)S(1)}, f32[40,128]{1,0:T(8,128)S(1)}, u32[]{:S(2)}, u32[]{:S(2)}) collective-permute-start(f32[40,128]{1,0:T(8,128)S(1)} %get-tuple-element.45), channel_id=1, source_target_pairs={{4,8},{12,16},{20,24},{28,32},{36,40},{44,48},{52,56},{60,64},{68,... | collective-permute-start | bytes 61448 | tf_op jit(solution)/shard_map/ppermute | solution.py:502
  70.8 4.9 %collective-permute-start.11 = (f32[40,128]{1,0:T(8,128)S(1)}, f32[40,128]{1,0:T(8,128)S(1)}, u32[]{:S(2)}, u32[]{:S(2)}) collective-permute-start(f32[40,128]{1,0:T(8,128)S(1)} %get-tuple-element.46), channel_id=1, source_target_pairs={{0,4},{8,12},{16,20},{24,28},{32,36},{40,44},{48,52},{56,60},{64,6... | collective-permute-start | bytes 61448 | tf_op jit(solution)/shard_map/ppermute | solution.py:502
  76.4 9.1 %collective-permute-start.13 = (f32[160,128]{1,0:T(8,128)S(1)}, f32[160,128]{1,0:T(8,128)S(1)}, u32[]{:S(2)}, u32[]{:S(2)}) collective-permute-start(f32[160,128]{1,0:T(8,128)S(1)} %shard_map.89.level), channel_id=1, source_target_pairs={{4,8},{12,16},{20,24},{28,32},{36,40},{44,48},{52,56},{60,64},{68,... | collective-permute-start | bytes 245768 | tf_op jit(solution)/shard_map/ppermute | solution.py:502
  79.9 5.5 %collective-permute-start.12 = (f32[160,128]{1,0:T(8,128)S(1)}, f32[160,128]{1,0:T(8,128)S(1)}, u32[]{:S(2)}, u32[]{:S(2)}) collective-permute-start(f32[160,128]{1,0:T(8,128)S(1)} %shard_map.89.level), channel_id=1, source_target_pairs={{0,4},{8,12},{16,20},{24,28},{32,36},{40,44},{48,52},{56,60},{64,6... | collective-permute-start | bytes 245768 | tf_op jit(solution)/shard_map/ppermute | solution.py:502
